TPU v7x, 1024 devices: a whole 4x4x32 slice. The times are simulated.
1024 devices in a mesh: section: 2 (over y_lo), tensor: 8 (over y_hi, x), dp: 64 (over z, core).
Axes of the slice: x: 4, y: 4 (y_hi: 2, y_lo: 2; y = y_hi * 2 + y_lo), z: 32, core: 2. Of those that a mesh axis runs over, the one named last changes fastest.
Arguments:
- cotangent: bfloat16 [2, 64, 128, 2048], P('section', 'dp', 'tensor'), may hold values from -6 to 6
- saved_input: bfloat16 [2, 2, 2, 64, 128, 2048], P(None, 'section', None, 'dp', 'tensor'), may hold values from -6 to 6
- saved_normed: bfloat16 [2, 2, 2, 64, 128, 2048], P(None, 'section', None, 'dp'), may hold values from -16 to 16
- saved_query: bfloat16 [2, 2, 2, 64, 128, 2048], P(None, 'section', None, 'dp', None, 'tensor'), may hold values from -6 to 6
- saved_keyval: bfloat16 [2, 2, 2, 64, 128, 8, 128], P(None, 'section', None, 'dp', None, 'tensor'), may hold values from -6 to 6
- norm_gain: float32 [2, 2, 2048], P(None, 'section'), may hold values from 0.5 to 1.5
- w_query: bfloat16 [2, 2, 2048, 2048], P(None, 'section', None, 'tensor'), may hold values from -0.125 to 0.125
- w_keyval: bfloat16 [2, 2, 2048, 8, 128], P(None, 'section', None, 'tensor'), may hold values from -0.125 to 0.125
- w_output: bfloat16 [2, 2, 2048, 2048], P(None, 'section', 'tensor'), may hold values from -0.125 to 0.125
Outputs:
- input_grad: bfloat16 [2, 64, 128, 2048], P('section', 'dp', 'tensor')
- keyval_grad: float32 [2, 2, 2048, 8, 128], P(None, 'section', 'dp', 'tensor')
All inputs are finite; a program needn't handle non-finite values.
Results may differ from a plain program's by a relative error of at most 0.035.
Values may be sent and summed in bfloat16 or wider, within the bound.
A program may use at most 64 MiB of HBM per device.

v0:
```python
import jax
import jax.numpy as jnp
from jax import lax
from jax.sharding import PartitionSpec as P


def from_behind(value, axis, steps):
    count = lax.axis_size(axis)
    pairs = [(source, (source + steps) % count) for source in range(count)]
    return lax.ppermute(value, axis, pairs)


def attend(query, keyval):
    n_batch, n_rows, query_width = query.shape
    kv_heads = keyval.shape[2]
    head_size = keyval.shape[3] // 2
    groups = query_width // (kv_heads * head_size)
    query_f = query.astype(jnp.float32).reshape(n_batch, n_rows, kv_heads, groups, head_size)
    key_rows = keyval[..., :head_size].astype(jnp.float32)
    values = keyval[..., head_size:].astype(jnp.float32)
    scores = jnp.einsum("bqhgd,bkhd->bhgqk", query_f, key_rows) * head_size ** (-0.5)
    places = jnp.arange(n_rows)
    causal = places[:, None] >= places[None, :]
    scores = jnp.where(causal, scores, -1e30)
    highest = lax.stop_gradient(jnp.max(scores, axis=-1, keepdims=True))
    weights = jnp.exp(scores - highest)
    shares = (weights / jnp.sum(weights, axis=-1, keepdims=True)).astype(jnp.bfloat16)
    mixture = jnp.einsum("bhgqk,bkhd->bqhgd", shares.astype(jnp.float32), values)
    return mixture.reshape(n_batch, n_rows, query_width).astype(jnp.bfloat16)


def normalize(values, gain_row):
    mean_sq = jnp.mean(values * values, axis=-1, keepdims=True)
    return values * lax.rsqrt(mean_sq + 1e-05) * gain_row


def rounded(term):
    return lax.optimization_barrier(term.astype(jnp.bfloat16)).astype(jnp.float32)


def select_slot(stash, slot, micro_idx):
    block = lax.dynamic_index_in_dim(stash[:, 0, :, 0], slot, 0, keepdims=False)
    return lax.dynamic_index_in_dim(block, micro_idx, 0, keepdims=False)


def slot_gradient(saved_normed, slot, kv_rows):
    normed_pair = saved_normed[slot, 0, :, 0]
    ordered = jnp.stack([kv_rows[1], kv_rows[0]])
    return jnp.einsum("msd,msk->dk", normed_pair, ordered, preferred_element_type=jnp.float32)


def on_device(
    cotangent,
    saved_input,
    saved_normed,
    saved_query,
    saved_keyval,
    norm_gain,
    w_query,
    w_keyval,
    w_output,
):
    section_index = lax.axis_index("section")
    at_front = section_index == 0
    shard_rows = cotangent.shape[2]
    model_width = cotangent.shape[3]
    full_rows = saved_normed.shape[4]
    query_width = w_query.shape[3]
    kv_heads = w_keyval.shape[3]
    kv_width = w_keyval.shape[4]
    kv_span = kv_heads * kv_width
    received = cotangent[0, 0]
    last_grad = received
    kv_store = []
    for step in range(5):
        offset = step - 1 + section_index
        is_valid = (offset >= 0) & (offset <= 3)
        safe_offset = jnp.clip(offset, 0, 3)
        slot = 1 - safe_offset // 2
        micro_idx = 1 - safe_offset % 2
        incoming = received
        gain_row = lax.dynamic_index_in_dim(norm_gain[:, 0], slot, 0, keepdims=False)
        w_out = lax.dynamic_index_in_dim(w_output[:, 0], slot, 0, keepdims=False)
        w_q = lax.dynamic_index_in_dim(w_query[:, 0], slot, 0, keepdims=False)
        w_kv = lax.dynamic_index_in_dim(w_keyval[:, 0], slot, 0, keepdims=False).reshape(
            model_width, kv_span
        )
        stored_x = select_slot(saved_input, slot, micro_idx)
        query = select_slot(saved_query, slot, micro_idx)
        keyval = select_slot(saved_keyval, slot, micro_idx)
        piece = lax.all_gather(incoming, "tensor", axis=0, tiled=True)
        d_attn = lax.cond(
            is_valid,
            lambda: jnp.einsum(
                "rd,ad->ra", piece, w_out, preferred_element_type=jnp.float32
            ).astype(jnp.bfloat16),
            lambda: jnp.zeros((piece.shape[0], query_width), jnp.bfloat16),
        )

        def backward_heads():
            _, pull = jax.vjp(attend, query[None], keyval[None])
            d_query, d_keyval = pull(d_attn[None])
            return (d_query[0], d_keyval[0].reshape(full_rows, kv_span))

        def skip_heads():
            return (
                jnp.zeros((full_rows, query_width), jnp.bfloat16),
                jnp.zeros((full_rows, kv_span), jnp.bfloat16),
            )

        d_query, d_flat = lax.cond(is_valid, backward_heads, skip_heads)
        kv_store.append(d_flat)
        piece_q = d_query
        piece_kv = d_flat

        def live():
            total = jnp.einsum("ra,da->rd", piece_q, w_q, preferred_element_type=jnp.float32)
            total = total + jnp.einsum(
                "rk,dk->rd", piece_kv, w_kv, preferred_element_type=jnp.float32
            )
            return rounded(total)

        d_normed = lax.psum_scatter(
            lax.cond(
                is_valid,
                live,
                lambda: jnp.zeros((lax.axis_size("tensor") * shard_rows, model_width), jnp.float32),
            ).astype(jnp.bfloat16),
            "tensor",
            scatter_dimension=0,
            tiled=True,
        ).astype(jnp.float32)
        _, pull_norm = jax.vjp(
            lambda values: normalize(values, gain_row), stored_x.astype(jnp.float32)
        )
        d_input = pull_norm(d_normed)[0]
        outgoing = (incoming.astype(jnp.float32) + d_input).astype(jnp.bfloat16)
        if step < 4:
            received = from_behind(jnp.where(is_valid, outgoing, incoming), "section", 1)
        else:
            last_grad = outgoing
    input_grad = jnp.where(at_front, last_grad, received)
    all_rows = jnp.stack(kv_store)
    slot_zero_rows = lax.dynamic_slice_in_dim(all_rows, 3 - section_index, 2, 0)
    slot_one_rows = lax.dynamic_slice_in_dim(all_rows, 1 - section_index, 2, 0)
    grad_sums = jnp.stack(
        [
            slot_gradient(saved_normed, 0, slot_zero_rows),
            slot_gradient(saved_normed, 1, slot_one_rows),
        ]
    )
    summed = lax.psum_scatter(grad_sums, "dp", scatter_dimension=1, tiled=True)
    keyval_grad = summed.reshape(2, 1, summed.shape[1], kv_heads, kv_width)
    return (input_grad[None, None], keyval_grad)


def solution(mesh):
    in_specs = (
        P("section", "dp", "tensor", None),
        P(None, "section", None, "dp", "tensor", None),
        P(None, "section", None, "dp", None, None),
        P(None, "section", None, "dp", None, "tensor"),
        P(None, "section", None, "dp", None, "tensor", None),
        P(None, "section", None),
        P(None, "section", None, "tensor"),
        P(None, "section", None, "tensor", None),
        P(None, "section", "tensor", None),
    )
    out_specs = (P("section", "dp", "tensor", None), P(None, "section", "dp", "tensor", None))
    return jax.shard_map(
        on_device, mesh=mesh, in_specs=in_specs, out_specs=out_specs, check_vma=False
    )
```

profile of v0, /device:TPU:2, one launch (start us, length us, event | category | flops | bytes accessed | tf_op | source)
XLA Modules:
  0.0 1265.6 jit_solution(16023779884705601434)
XLA Ops:
  7.3 42.9 %all-gather = bf16[1,1,128,2048]{3,2,1,0:T(8,128)(2,1)S(1)} all-gather(bf16[1,1,16,2048]{3,2,1,0:T(8,128)(2,1)} %param.39), channel_id=2, replica_groups=mesh['section'=2,'tensor'=8,'dp'=64] {'tensor'}, dimensions={2}, use_global_device_ids=true | all-gather | bytes 589824 | tf_op jit(solution)/shard_map/all_gather | solution.py:91
  53.6 2.2 copy.91
  56.6 114.8 %reduce-scatter.6.cloned.1.call-done = bf16[16,2048]{1,0:T(8,128)(2,1)} async-done(((bf16[128,2048]{1,0:T(8,128)(2,1)}), bf16[16,2048]{1,0:T(8,128)(2,1)}) %reduce-scatter.6.cloned.1.call-update) | async-done | bytes 65552 | tf_op jit(solution)/shard_map/reduce_scatter | solution.py:123
  174.9 2.4 collective-permute-start
  177.3 4.0 collective-permute-done
  181.4 35.3 %all_gather.16 = bf16[128,2048]{1,0:T(8,128)(2,1)} all-gather(bf16[16,2048]{1,0:T(8,128)(2,1)} %collective-permute-done), channel_id=1, replica_groups=mesh['section'=2,'tensor'=8,'dp'=64] {'tensor'}, dimensions={0}, use_global_device_ids=true | all-gather | bytes 589824 | tf_op jit(solution)/shard_map/all_gather | solution.py:91
  218.8 6.8 conditional.19
  226.1 3.4 conditional.20
  231.7 107.6 %reduce-scatter.8.cloned.1.call-done = bf16[16,2048]{1,0:T(8,128)(2,1)} async-done(((bf16[128,2048]{1,0:T(8,128)(2,1)}), bf16[16,2048]{1,0:T(8,128)(2,1)}) %reduce-scatter.8.cloned.1.call-update) | async-done | bytes 65552 | tf_op jit(solution)/shard_map/reduce_scatter | solution.py:123
  342.5 2.5 collective-permute-start.1
  345.0 4.0 collective-permute-done.1
  349.0 35.4 %all_gather.17 = bf16[128,2048]{1,0:T(8,128)(2,1)} all-gather(bf16[16,2048]{1,0:T(8,128)(2,1)} %collective-permute-done.1), channel_id=1, replica_groups=mesh['section'=2,'tensor'=8,'dp'=64] {'tensor'}, dimensions={0}, use_global_device_ids=true | all-gather | bytes 589824 | tf_op jit(solution)/shard_map/all_gather | solution.py:91
  386.4 6.8 conditional.22
  393.8 3.4 conditional.23
  399.4 107.6 %reduce-scatter.10.cloned.1.call-done = bf16[16,2048]{1,0:T(8,128)(2,1)} async-done(((bf16[128,2048]{1,0:T(8,128)(2,1)}), bf16[16,2048]{1,0:T(8,128)(2,1)}) %reduce-scatter.10.cloned.1.call-update) | async-done | bytes 65552 | tf_op jit(solution)/shard_map/reduce_scatter | solution.py:123
  510.3 2.4 collective-permute-start.2
  512.8 4.0 collective-permute-done.2
  516.8 35.3 %all_gather.18 = bf16[128,2048]{1,0:T(8,128)(2,1)} all-gather(bf16[16,2048]{1,0:T(8,128)(2,1)} %collective-permute-done.2), channel_id=1, replica_groups=mesh['section'=2,'tensor'=8,'dp'=64] {'tensor'}, dimensions={0}, use_global_device_ids=true | all-gather | bytes 589824 | tf_op jit(solution)/shard_map/all_gather | solution.py:91
  552.1 2.1 conditional.24
  552.1 2.1 fusion.78
  554.2 6.8 conditional.25
  561.6 3.4 conditional.26
  571.3 103.4 %reduce-scatter.12.cloned.1.call-done = bf16[16,2048]{1,0:T(8,128)(2,1)} async-done(((bf16[128,2048]{1,0:T(8,128)(2,1)}), bf16[16,2048]{1,0:T(8,128)(2,1)}) %reduce-scatter.12.cloned.1.call-update) | async-done | bytes 65552 | tf_op jit(solution)/shard_map/reduce_scatter | solution.py:123
  676.8 2.5 collective-permute-start.3
  680.6 2.3 collective-permute-done.3
  682.9 35.1 %all_gather.19 = bf16[128,2048]{1,0:T(8,128)(2,1)} all-gather(bf16[16,2048]{1,0:T(8,128)(2,1)S(1)} %collective-permute-done.3), channel_id=1, replica_groups=mesh['section'=2,'tensor'=8,'dp'=64] {'tensor'}, dimensions={0}, use_global_device_ids=true | all-gather | bytes 589824 | tf_op jit(solution)/shard_map/all_gather | solution.py:91
  718.0 2.1 conditional.27
  720.1 6.8 conditional.28
  729.3 2.3 copy.114
  733.2 2.4 conditional.29
  739.6 404.8 %all-reduce.13.cloned.1.call-done = f32[2,2048,128]{2,0,1:T(2,128)} async-done(((f32[2,2048,128]{2,0,1:T(2,128)}), f32[2,2048,128]{2,0,1:T(2,128)}) %all-reduce.13.cloned.1.call-update) | async-done | bytes 2097168
  1145.8 110.4 %reduce-scatter.14.cloned.1.call-done = bf16[16,2048]{1,0:T(8,128)(2,1)} async-done(((bf16[128,2048]{1,0:T(8,128)(2,1)}), bf16[16,2048]{1,0:T(8,128)(2,1)}) %reduce-scatter.14.cloned.1.call-update) | async-done | bytes 65552 | tf_op jit(solution)/shard_map/reduce_scatter | solution.py:123
  (196 shorter events, 92.0 us)
Async XLA Ops:
  7.2 43.7 %copy-start.5 = (bf16[2,1,2,1,128,1,128]{6,4,5,3,2,1,0:T(8,128)(2,1)S(1)}, bf16[2,1,2,1,128,1,128]{6,4,5,3,2,1,0:T(8,128)(2,1)}, u32[]{:S(2)}) copy-start(bf16[2,1,2,1,128,1,128]{6,4,5,3,2,1,0:T(8,128)(2,1)} %param.43) | copy-start | bytes 393220
  7.2 43.7 %copy-start.4 = (bf16[2,1,2,1,128,256]{5,4,3,2,1,0:T(8,128)(2,1)S(1)}, bf16[2,1,2,1,128,256]{5,4,3,2,1,0:T(8,128)(2,1)}, u32[]{:S(2)}) copy-start(bf16[2,1,2,1,128,256]{5,4,3,2,1,0:T(8,128)(2,1)} %param.42) | copy-start | bytes 786436
  7.2 164.2 %reduce-scatter.6.cloned.1.call-start = ((), (), s32[]{:S(2)}) async-start(), calls=%async_computation.5 | async-start | bytes 589824 | tf_op jit(solution)/shard_map/reduce_scatter | solution.py:123
  50.9 1.9 copy-start.3
  50.9 1.8 copy-start.13
  52.7 3.2 copy-start.36
  53.6 163.1 %copy-start = (bf16[2,1,256,2048]{3,2,1,0:T(8,128)(2,1)S(1)}, bf16[2,1,256,2048]{3,2,1,0:T(8,128)(2,1)}, u32[]{:S(2)}) copy-start(bf16[2,1,256,2048]{3,2,1,0:T(8,128)(2,1)} %param.47) | copy-start | bytes 6291460
  55.8 283.4 %reduce-scatter.8.cloned.1.call-start = ((), (), s32[]{:S(2)}) async-start(), calls=%async_computation.6 | async-start | bytes 589824 | tf_op jit(solution)/shard_map/reduce_scatter | solution.py:123
  174.9 6.5 collective-permute-start
  221.9 3.3 copy-start.9
  221.9 3.5 copy-start.31
  225.5 113.7 %copy-start.40 = (f32[1,1,2048]{2,1,0:T(1,128)S(1)}, f32[1,1,2048]{2,1,0:T(1,128)}, u32[]{:S(2)}) copy-start(f32[1,1,2048]{2,1,0:T(1,128)} %get-tuple-element.800) | copy-start | bytes 24580
  231.6 275.3 %reduce-scatter.10.cloned.1.call-start = ((), (), s32[]{:S(2)}) async-start(), calls=%async_computation.7 | async-start | bytes 589824 | tf_op jit(solution)/shard_map/reduce_scatter | solution.py:123
  342.5 6.5 collective-permute-start.1
  389.5 3.3 copy-start.10
  389.5 3.5 copy-start.32
  393.2 113.7 %copy-start.39 = (f32[1,1,2048]{2,1,0:T(1,128)S(1)}, f32[1,1,2048]{2,1,0:T(1,128)}, u32[]{:S(2)}) copy-start(f32[1,1,2048]{2,1,0:T(1,128)} %get-tuple-element.799) | copy-start | bytes 24580
  394.5 1.7 copy-start.21
  399.3 275.4 %reduce-scatter.12.cloned.1.call-start = ((), (), s32[]{:S(2)}) async-start(), calls=%async_computation.8 | async-start | bytes 589824 | tf_op jit(solution)/shard_map/reduce_scatter | solution.py:123
  510.3 6.5 collective-permute-start.2
  557.3 3.3 copy-start.11
  557.3 3.5 copy-start.33
  561.0 113.7 %copy-start.38 = (f32[1,1,2048]{2,1,0:T(1,128)S(1)}, f32[1,1,2048]{2,1,0:T(1,128)}, u32[]{:S(2)}) copy-start(f32[1,1,2048]{2,1,0:T(1,128)} %get-tuple-element.802) | copy-start | bytes 24580
  567.1 577.3 %all-reduce.13.cloned.1.call-start = ((), (), s32[]{:S(2)}) async-start(), calls=%async_computation.10 | async-start | bytes 4194304
  676.8 6.2 collective-permute-start.3
  682.9 35.1 %copy-start.34 = (bf16[16,2048]{1,0:T(8,128)(2,1)}, bf16[16,2048]{1,0:T(8,128)(2,1)S(1)}, u32[]{:S(2)}) copy-start(bf16[16,2048]{1,0:T(8,128)(2,1)S(1)} %collective-permute-done.3) | copy-start | bytes 196612
  720.1 8.3 copy-start.7
  722.6 3.2 copy-start.12
  731.6 524.6 %reduce-scatter.14.cloned.1.call-start = ((), (), s32[]{:S(2)}) async-start(), calls=%async_computation.9 | async-start | bytes 589824 | tf_op jit(solution)/shard_map/reduce_scatter | solution.py:123
  733.2 523.0 %copy-start.6 = (bf16[2,1,2,1,16,2048]{5,4,3,2,1,0:T(8,128)(2,1)S(1)}, bf16[2,1,2,1,16,2048]{5,4,3,2,1,0:T(8,128)(2,1)}, u32[]{:S(2)}) copy-start(bf16[2,1,2,1,16,2048]{5,4,3,2,1,0:T(8,128)(2,1)} %param.40) | copy-start | bytes 786436
  733.2 523.0 %copy-start.37 = (f32[1,1,2048]{2,1,0:T(1,128)S(1)}, f32[1,1,2048]{2,1,0:T(1,128)}, u32[]{:S(2)}) copy-start(f32[1,1,2048]{2,1,0:T(1,128)} %get-tuple-element.798) | copy-start | bytes 24580
  733.2 524.0 %copy-start.35 = (bf16[16,2048]{1,0:T(8,128)(2,1)S(1)}, bf16[16,2048]{1,0:T(8,128)(2,1)}, u32[]{:S(2)}) copy-start(bf16[16,2048]{1,0:T(8,128)(2,1)} %copy-done.34) | copy-start | bytes 196612
  (14 other events, 12.7 us)
Sparse Core Ops, SparseCore 0:
  56.0 115.4 reduce-scatter.5
  231.7 107.4 reduce-scatter.7
  399.4 107.4 reduce-scatter.9
  567.2 107.4 reduce-scatter.11
  731.8 412.6 all-reduce.12
  1150.8 105.3 reduce-scatter.13
where the time goes:
time: 1270 us
  waiting for transfers between devices  963 us (76%)
  blocking collectives  184 us (14%)
  local copies, waits for them, and re-layouts  45.7 us (4%)
  matrix products  31.7 us (2%)
  other arithmetic  15.7 us (1%)
  between operations  15.1 us (1%)
    reduce_scatter x5, waiting for transfers between devices, on_device(): lax.psum_scatter(lax.cond(is_valid, live, lambda: jnp.zeros((lax.axis_siz...  544 us
    unnamed x7, waiting for transfers between devices  405 us
    all_gather x5, blocking collectives, on_device(): piece = lax.all_gather(incoming, 'tensor', axis=0, tiled=True)  184 us
  transfers between devices with their start and end apart: 10, of which 10 were waited for; matrix products, arithmetic and copies ran while one was open for 1% of the time, Pallas kernels for 0%

commit v1 on v0

v1 whole, which is shorter than its diff:
```python
import functools

import jax
import jax.numpy as jnp
from jax import lax
from jax.experimental import pallas as pl
from jax.experimental.pallas import tpu as pltpu
from jax.sharding import PartitionSpec as P

MESH = pl.DeviceIdType.MESH
BF16 = jnp.bfloat16
F32 = jnp.float32
NT = (((1,), (1,)), ((), ()))
TN = (((0,), (0,)), ((), ()))
NN = (((1,), (0,)), ((), ()))
NEAR = 4


def dot(a, b, dims):
    return lax.dot_general(a, b, dims, preferred_element_type=F32)


def attention_grads(query, keyval, d_attn):
    rows, q_width = query.shape
    head = keyval.shape[1] // 2
    n_heads = q_width // head
    scale = head**-0.5
    low = lax.broadcasted_iota(jnp.int32, (rows, 2 * head), 1) < head
    kv = keyval.astype(F32)
    vk = pltpu.roll(kv, head, 1)
    zero = jnp.zeros((rows, 2 * head), BF16)
    k_low = jnp.where(low, kv * scale, 0.0).astype(BF16)
    k_high = jnp.where(low, 0.0, vk * scale).astype(BF16)
    v_low = jnp.where(low, vk, 0.0).astype(BF16)
    v_high = jnp.where(low, 0.0, kv).astype(BF16)

    def spread(even, odd):
        parts = []
        for i in range(n_heads):
            own = odd if i % 2 else even
            parts.append(
                jnp.concatenate(
                    [own if i // 2 == p else zero for p in range(n_heads // 2)], axis=1
                )
            )
        return jnp.concatenate(parts, axis=0)

    keys = spread(k_low, k_high)
    values = spread(v_low, v_high)
    scores = dot(keys, query, NT)
    d_share = dot(values, d_attn, NT)
    causal = lax.broadcasted_iota(jnp.int32, (rows, rows), 0) <= lax.broadcasted_iota(
        jnp.int32, (rows, rows), 1
    )
    shares, d_scores = [], []
    for i in range(n_heads):
        s = jnp.where(causal, scores[i * rows : (i + 1) * rows], -1e30)
        e = jnp.exp(s - jnp.max(s, axis=0, keepdims=True))
        p = e / jnp.sum(e, axis=0, keepdims=True)
        dp = d_share[i * rows : (i + 1) * rows]
        ds = p * (dp - jnp.sum(p * dp, axis=0, keepdims=True))
        shares.append(p.astype(BF16))
        d_scores.append(ds.astype(BF16))
    d_query = dot(jnp.concatenate(d_scores, axis=0), keys, TN)

    def by_parity(blocks):
        return jnp.concatenate(
            [jnp.concatenate(blocks[0::2], axis=1), jnp.concatenate(blocks[1::2], axis=1)], axis=0
        )

    def stacked(array):
        return jnp.concatenate(
            [array[:, p * 2 * head : (p + 1) * 2 * head] for p in range(n_heads // 2)], axis=0
        )

    dk = dot(by_parity(d_scores), stacked(query), NN) * scale
    dv = dot(by_parity(shares), stacked(d_attn), NN)
    d_keyval = jnp.where(low, dk[:rows], dv[rows:]) + pltpu.roll(
        jnp.where(low, dv[:rows], dk[rows:]), head, 1
    )
    return d_query.astype(BF16), d_keyval.astype(BF16)


def kernel(
    n_tensor,
    n_dp,
    cot_hbm,
    xin_hbm,
    xn_hbm,
    q_hbm,
    kv_hbm,
    gain_hbm,
    wq_hbm,
    wkv_hbm,
    wo_hbm,
    out_ref,
    grad_ref,
    xin,
    xn,
    q,
    kv,
    gain,
    wq,
    wkv,
    wo,
    gathered,
    parts,
    landed,
    outs,
    final,
    dkv,
    turned,
    core_out,
    core_own,
    core_in,
    z1_out,
    z1_in,
    z2_out,
    z2_in,
    load_sem,
    ag_send,
    ag_recv,
    out_send,
    rs_send,
    rs_recv,
    fin_send,
    fin_recv,
    core_send,
    core_recv,
    z1_send,
    z1_recv,
    z2_send,
    z2_recv,
    go_sem,
    token_sem,
):
    s = lax.axis_index("section")
    t = lax.axis_index("tensor")
    d = lax.axis_index("dp")
    z, core = d // 2, d % 2
    n_z = n_dp // 2
    n_far = n_z // NEAR
    zi, zg = z % NEAR, z // NEAR
    shard = outs.shape[1]
    n_rows = q.shape[2]
    chunk = grad_ref.shape[1]
    first = s == 1

    def tensor_peer(j):
        return lax.rem(t + j, n_tensor)

    def near_peer(j):
        return (zg * NEAR + lax.rem(zi + j, NEAR)) * 2 + core

    def far_peer(j):
        return (lax.rem(zg + j, n_far) * NEAR + zi) * 2 + core

    barrier = pltpu.get_barrier_semaphore()

    def hello(device):
        pl.semaphore_signal(barrier, inc=1, device_id=device, device_id_type=MESH)

    for j in range(1, n_tensor):
        hello({"tensor": tensor_peer(j)})
    for j in range(n_tensor):
        hello({"section": 1 - s, "tensor": tensor_peer(j)})
    hello({"dp": z * 2 + 1 - core})
    for j in range(1, NEAR):
        hello({"dp": near_peer(j)})
    for j in (1, n_far - 1):
        hello({"dp": far_peer(j)})

    loads = [
        pltpu.make_async_copy(src, dst, load_sem.at[i])
        for i, (src, dst) in enumerate(
            [
                (wo_hbm, wo),
                (q_hbm, q),
                (kv_hbm, kv),
                (wq_hbm, wq),
                (wkv_hbm, wkv),
                (xin_hbm, xin),
                (gain_hbm, gain),
                (xn_hbm, xn),
            ]
        )
    ]
    for load in loads:
        load.start()

    pl.semaphore_wait(barrier, 2 * n_tensor - 1 + 1 + NEAR - 1 + 2)

    def rows_of(index):
        return pl.ds(pl.multiple_of(index * shard, shard), shard)

    def gather_copy(src, item, j, section):
        return pltpu.make_async_remote_copy(
            src_ref=src,
            dst_ref=gathered.at[item, rows_of(t)],
            send_sem=ag_send.at[item, j],
            recv_sem=ag_recv.at[item, j],
            device_id={"section": section, "tensor": tensor_peer(j)},
            device_id_type=MESH,
        )

    def reply_copy(k, item, j):
        return pltpu.make_async_remote_copy(
            src_ref=outs.at[k],
            dst_ref=gathered.at[item, rows_of(t)],
            send_sem=out_send.at[k, j],
            recv_sem=ag_recv.at[item, j],
            device_id={"section": 1 - s, "tensor": tensor_peer(j)},
            device_id_type=MESH,
        )

    def own_shard_copy():
        return pltpu.make_async_copy(cot_hbm, gathered.at[0, rows_of(t)], ag_recv.at[0, 0])

    def reduce_copy(k, j):
        return pltpu.make_async_remote_copy(
            src_ref=parts.at[k, rows_of(tensor_peer(j))],
            dst_ref=landed.at[k, rows_of(j)],
            send_sem=rs_send.at[k, j],
            recv_sem=rs_recv.at[k, j],
            device_id={"tensor": tensor_peer(j)},
            device_id_type=MESH,
        )

    def final_copy():
        return pltpu.make_async_remote_copy(
            src_ref=outs.at[2],
            dst_ref=final,
            send_sem=fin_send,
            recv_sem=fin_recv,
            device_id={"section": 1 - s},
            device_id_type=MESH,
        )

    def core_copy(slot):
        return pltpu.make_async_remote_copy(
            src_ref=core_out.at[slot],
            dst_ref=core_in.at[slot],
            send_sem=core_send.at[slot],
            recv_sem=core_recv.at[slot],
            device_id={"dp": z * 2 + 1 - core},
            device_id_type=MESH,
        )

    def near_copy(slot, j):
        return pltpu.make_async_remote_copy(
            src_ref=z1_out.at[slot, lax.rem(zi + j, NEAR)],
            dst_ref=z1_in.at[slot, j],
            send_sem=z1_send.at[slot, j],
            recv_sem=z1_recv.at[slot, j],
            device_id={"dp": near_peer(j)},
            device_id_type=MESH,
        )

    def far_copy(slot, j):
        return pltpu.make_async_remote_copy(
            src_ref=z2_out.at[slot, lax.rem(zg + j, n_far)],
            dst_ref=z2_in.at[slot, j],
            send_sem=z2_send.at[slot, j],
            recv_sem=z2_recv.at[slot, j],
            device_id={"dp": far_peer(j)},
            device_id_type=MESH,
        )

    def greet(round_index):
        for j in (1, n_far - 1):
            pl.semaphore_signal(
                token_sem.at[round_index],
                inc=1,
                device_id={"dp": far_peer(j)},
                device_id_type=MESH,
            )

    def greeted(round_index):
        pl.semaphore_wait(token_sem.at[round_index], 2)

    def turn(slot):
        def block(b, carry):
            columns = pl.ds(pl.multiple_of(b * 128, 128), 128)
            for place in range(2):
                flat = xn[slot, 1 - place, :, columns].T
                for i in range(128 // chunk):
                    owner = b * (128 // chunk) + i
                    oz, oc = owner // 2, owner % 2
                    where = (oz % NEAR) * n_far + oz // NEAR
                    turned[
                        slot,
                        oc,
                        pl.ds(pl.multiple_of(where * chunk, chunk), chunk),
                        place * n_rows : (place + 1) * n_rows,
                    ] = flat[i * chunk : (i + 1) * chunk]
            return carry

        lax.fori_loop(0, xn.shape[3] // 128, block, 0)

    def gradient(slot):
        rows = dkv[slot]

        def theirs(b, carry):
            span = pl.ds(pl.multiple_of(b * 256, 256), 256)
            core_out[slot, span] = dot(turned[slot, 1 - core, span], rows, NN).astype(BF16)
            return carry

        def ours(b, carry):
            span = pl.ds(pl.multiple_of(b * 256, 256), 256)
            core_own[slot, span] = dot(turned[slot, core, span], rows, NN)
            return carry

        count = core_out.shape[1] // 256
        lax.fori_loop(0, count, theirs, 0)
        core_copy(slot).start()
        lax.fori_loop(0, count, ours, 0)

    def near_phase(slot):
        core_copy(slot).wait_recv()
        block = n_far * chunk
        for i in range(NEAR):
            span = slice(i * block, (i + 1) * block)
            total = core_own[slot, span] + core_in[slot, span].astype(F32)
            core_own[slot, span] = total
            z1_out[slot, i] = total.astype(BF16)
        for j in range(1, NEAR):
            near_copy(slot, j).start()

    def far_phase(slot):
        block = n_far * chunk
        total = core_own[slot, pl.ds(pl.multiple_of(zi * block, block), block)]
        for j in range(1, NEAR):
            near_copy(slot, j).wait_recv()
            total = total + z1_in[slot, j].astype(F32)
        for g in range(n_far):
            piece = total[g * chunk : (g + 1) * chunk]
            z2_out[slot, g] = piece.astype(BF16)

            @pl.when(g == zg)
            def _():
                grad_ref[slot] = piece

        for j in range(1, n_far):
            far_copy(slot, j).start()

    def last_phase(slot):
        total = grad_ref[slot]
        for j in range(1, n_far):
            far_copy(slot, j).wait_recv()
            total = total + z2_in[slot, j].astype(F32)
        grad_ref[slot] = total

    @pl.when(first)
    def _():
        for j in range(1, n_tensor):
            gather_copy(cot_hbm, 0, j, s).start()
        own_shard_copy().start()

    greet(0)
    for load in loads:
        load.wait()

    @pl.when(jnp.logical_not(first))
    def _():
        pl.semaphore_wait(go_sem, 1)
        for j in range(n_tensor):
            gather_copy(cot_hbm, 1, j, 1 - s).start()

    def step(k, carry):
        slot = 1 - k // 2
        place = k % 2
        micro = 1 - place
        tail = jnp.logical_and(k == 3, jnp.logical_not(first))
        for j in range(n_tensor):
            gather_copy(outs.at[0], k, j, s).wait_recv()

        @pl.when(jnp.logical_and(first, k == 0))
        def _():
            pl.semaphore_signal(go_sem, inc=1, device_id={"section": 1 - s}, device_id_type=MESH)

        d_attn = dot(gathered[k], wo[slot], NT).astype(BF16)
        d_query, d_keyval = attention_grads(q[slot, micro], kv[slot, micro], d_attn)
        dkv[slot, pl.ds(pl.multiple_of(place * n_rows, n_rows), n_rows)] = d_keyval

        @pl.when(tail)
        def _():
            gradient(0)

        parts[k] = (dot(d_query, wq[slot], NT) + dot(d_keyval, wkv[slot], NT)).astype(BF16)

        @pl.when(tail)
        def _():
            near_phase(0)

        for j in range(1, n_tensor):
            reduce_copy(k, j).start()

        @pl.when(place == 0)
        def _():
            turn(slot)

        @pl.when(jnp.logical_and(place == 1, jnp.logical_not(tail)))
        def _():
            gradient(slot)
            near_phase(slot)

        @pl.when(k < 2)
        def _():
            greeted(k)
            greet(k + 1)

        @pl.when(k == 2)
        def _():
            greeted(2)
            far_phase(1)

        @pl.when(tail)
        def _():
            far_phase(0)

        x = xin[slot, micro].astype(F32)
        mean_sq = jnp.mean(x * x, axis=-1, keepdims=True)
        r = lax.rsqrt(mean_sq + 1e-05)
        d_normed = parts[k, rows_of(t)].astype(F32)
        for j in range(1, n_tensor):
            reduce_copy(k, j).wait_recv()
            d_normed = d_normed + landed[k, j * shard : (j + 1) * shard].astype(F32)
        scaled = d_normed * gain[slot]
        along = jnp.mean(x * scaled, axis=-1, keepdims=True)
        d_input = r * scaled - x * (r * r * r * along)
        outs[k] = (gathered[k, rows_of(t)].astype(F32) + d_input).astype(BF16)

        @pl.when(first)
        def _():
            for j in range(n_tensor):
                reply_copy(k, k, j).start()

        @pl.when(jnp.logical_and(jnp.logical_not(first), k < 2))
        def _():
            for j in range(n_tensor):
                reply_copy(k, k + 2, j).start()

        @pl.when(jnp.logical_and(jnp.logical_not(first), k == 2))
        def _():
            final_copy().start()

        return carry

    lax.fori_loop(0, 4, step, 0)

    @pl.when(first)
    def _():
        far_phase(0)
        final_copy().wait_recv()
        out_ref[...] = final[...]
        for j in range(1, n_tensor):
            gather_copy(cot_hbm, 0, j, s).wait_send()
        for k in range(4):
            for j in range(n_tensor):
                reply_copy(k, k, j).wait_send()

    @pl.when(jnp.logical_not(first))
    def _():
        out_ref[...] = outs[3]
        final_copy().wait_send()
        for j in range(n_tensor):
            gather_copy(cot_hbm, 1, j, 1 - s).wait_send()
        for k in range(2):
            for j in range(n_tensor):
                reply_copy(k, k + 2, j).wait_send()

    last_phase(1)
    last_phase(0)
    for k in range(4):
        for j in range(1, n_tensor):
            reduce_copy(k, j).wait_send()
    for slot in range(2):
        core_copy(slot).wait_send()
        for j in range(1, NEAR):
            near_copy(slot, j).wait_send()
        for j in range(1, n_far):
            far_copy(slot, j).wait_send()


def on_device(
    n_tensor,
    n_dp,
    cotangent,
    saved_input,
    saved_normed,
    saved_query,
    saved_keyval,
    norm_gain,
    w_query,
    w_keyval,
    w_output,
):
    layers, _, micros, _, shard, width = saved_input.shape
    n_rows, q_width = saved_query.shape[4:]
    kv_width = w_keyval.shape[4]
    chunk = width // n_dp
    n_z = n_dp // 2
    n_far = n_z // NEAR
    items = layers * micros
    any_spec = pl.BlockSpec(memory_space=pl.ANY)
    vmem_spec = pl.BlockSpec(memory_space=pltpu.VMEM)
    dma = pltpu.SemaphoreType.DMA
    input_grad, keyval_grad = pl.pallas_call(
        functools.partial(kernel, n_tensor, n_dp),
        out_shape=(
            jax.ShapeDtypeStruct((shard, width), BF16),
            jax.ShapeDtypeStruct((layers, chunk, kv_width), F32),
        ),
        in_specs=[any_spec] * 9,
        out_specs=(vmem_spec, vmem_spec),
        scratch_shapes=[
            pltpu.VMEM((layers, micros, shard, width), BF16),
            pltpu.VMEM((layers, micros, n_rows, width), BF16),
            pltpu.VMEM((layers, micros, n_rows, q_width), BF16),
            pltpu.VMEM((layers, micros, n_rows, kv_width), BF16),
            pltpu.VMEM((layers, 1, width), F32),
            pltpu.VMEM((layers, width, q_width), BF16),
            pltpu.VMEM((layers, width, kv_width), BF16),
            pltpu.VMEM((layers, q_width, width), BF16),
            pltpu.VMEM((items, n_rows, width), BF16),
            pltpu.VMEM((items, n_rows, width), BF16),
            pltpu.VMEM((items, n_rows, width), BF16),
            pltpu.VMEM((items, shard, width), BF16),
            pltpu.VMEM((shard, width), BF16),
            pltpu.VMEM((layers, micros * n_rows, kv_width), BF16),
            pltpu.VMEM((layers, 2, width // 2, micros * n_rows), BF16),
            pltpu.VMEM((layers, width // 2, kv_width), BF16),
            pltpu.VMEM((layers, width // 2, kv_width), F32),
            pltpu.VMEM((layers, width // 2, kv_width), BF16),
            pltpu.VMEM((layers, NEAR, n_far * chunk, kv_width), BF16),
            pltpu.VMEM((layers, NEAR, n_far * chunk, kv_width), BF16),
            pltpu.VMEM((layers, n_far, chunk, kv_width), BF16),
            pltpu.VMEM((layers, n_far, chunk, kv_width), BF16),
            dma((8,)),
            dma((items, n_tensor)),
            dma((items, n_tensor)),
            dma((items, n_tensor)),
            dma((items, n_tensor)),
            dma((items, n_tensor)),
            dma(()),
            dma(()),
            dma((layers,)),
            dma((layers,)),
            dma((layers, NEAR)),
            dma((layers, NEAR)),
            dma((layers, n_far)),
            dma((layers, n_far)),
            pltpu.SemaphoreType.REGULAR,
            pltpu.SemaphoreType.REGULAR((3,)),
        ],
        compiler_params=pltpu.CompilerParams(
            collective_id=0, has_side_effects=True, vmem_limit_bytes=56 * 2**20
        ),
        name="backward",
    )(
        cotangent.reshape(shard, width),
        saved_input.reshape(layers, micros, shard, width),
        saved_normed.reshape(layers, micros, n_rows, width),
        saved_query.reshape(layers, micros, n_rows, q_width),
        saved_keyval.reshape(layers, micros, n_rows, kv_width),
        norm_gain,
        w_query.reshape(layers, width, q_width),
        w_keyval.reshape(layers, width, kv_width),
        w_output.reshape(layers, q_width, width),
    )
    return (
        input_grad[None, None],
        keyval_grad.reshape(layers, 1, chunk, 1, kv_width),
    )


def solution(mesh):
    in_specs = (
        P("section", "dp", "tensor", None),
        P(None, "section", None, "dp", "tensor", None),
        P(None, "section", None, "dp", None, None),
        P(None, "section", None, "dp", None, "tensor"),
        P(None, "section", None, "dp", None, "tensor", None),
        P(None, "section", None),
        P(None, "section", None, "tensor"),
        P(None, "section", None, "tensor", None),
        P(None, "section", "tensor", None),
    )
    out_specs = (P("section", "dp", "tensor", None), P(None, "section", "dp", "tensor", None))
    return jax.shard_map(
        functools.partial(on_device, mesh.shape["tensor"], mesh.shape["dp"]),
        mesh=mesh,
        in_specs=in_specs,
        out_specs=out_specs,
        check_vma=False,
    )
```

time: 1270 us -> 138 us (0.11)
  the two profiles are of different devices: /device:TPU:2 before, /device:TPU:96 now
where the time goes in v1:
time: 138 us; the launch traced here: 137 us
  Pallas kernels  134 us (97%)
  local copies, waits for them, and re-layouts  2.85 us (2%)
    pallas_call x1, Pallas kernels, on_device(): pl.pallas_call(functools.partial(kernel, n_tensor, n_dp), out_shape=(jax....  134 us
    unnamed x2, local copies, waits for them, and re-layouts  2.85 us

profile of v1, /device:TPU:96, one launch (start us, length us, event | category | flops | bytes accessed | tf_op | source)
XLA Modules:
  0.0 137.5 jit_solution(16037235476062002347)
XLA Ops:
  0.6 134.0 %backward.1 = (bf16[16,2048]{1,0:T(8,128)(2,1)}, f32[2,32,128]{2,1,0:T(8,128)}) custom-call(bf16[16,2048]{1,0:T(8,128)(2,1)} %bitcast.19, bf16[2,2,16,2048]{3,2,1,0:T(8,128)(2,1)} %bitcast.16, bf16[2,2,128,2048]{3,2,1,0:T(8,128)(2,1)} %bitcast.12, bf16[2,2,128,256]{3,2,1,0:T(8,128)(2,1)} %bitcast.17, bf16[2,2,128,128]{3,2,1,0:T(8,128)(2,1)} %bitcast.18, ...), custom_call_target="tpu_custom_call" | custom-call | tf_op jit(solution)/shard_map/backward/pallas_call | solution.py:508
  134.6 1.5 %copy.14 = bf16[1,1,16,2048]{3,2,1,0:T(8,128)(2,1)} copy(bf16[1,1,16,2048]{3,2,1,0:T(8,128)(2,1)} %bitcast.20) | data formatting | bytes 131072
  136.1 1.4 copy.15

commit v2 on v1

--- a/solution.py
+++ b/solution.py
@@ -20,65 +20,61 @@
     return lax.dot_general(a, b, dims, preferred_element_type=F32)
 
 
-def attention_grads(query, keyval, d_attn):
+def attention_grads(query, keyval, d_attn, offset):
     rows, q_width = query.shape
-    head = keyval.shape[1] // 2
-    n_heads = q_width // head
+    n_keys, lanes = keyval.shape
+    head = lanes // 2
     scale = head**-0.5
-    low = lax.broadcasted_iota(jnp.int32, (rows, 2 * head), 1) < head
+    low = lax.broadcasted_iota(jnp.int32, (n_keys, lanes), 1) < head
     kv = keyval.astype(F32)
     vk = pltpu.roll(kv, head, 1)
-    zero = jnp.zeros((rows, 2 * head), BF16)
-    k_low = jnp.where(low, kv * scale, 0.0).astype(BF16)
-    k_high = jnp.where(low, 0.0, vk * scale).astype(BF16)
-    v_low = jnp.where(low, vk, 0.0).astype(BF16)
-    v_high = jnp.where(low, 0.0, kv).astype(BF16)
-
-    def spread(even, odd):
-        parts = []
-        for i in range(n_heads):
-            own = odd if i % 2 else even
-            parts.append(
-                jnp.concatenate(
-                    [own if i // 2 == p else zero for p in range(n_heads // 2)], axis=1
-                )
-            )
-        return jnp.concatenate(parts, axis=0)
-
-    keys = spread(k_low, k_high)
-    values = spread(v_low, v_high)
-    scores = dot(keys, query, NT)
-    d_share = dot(values, d_attn, NT)
-    causal = lax.broadcasted_iota(jnp.int32, (rows, rows), 0) <= lax.broadcasted_iota(
-        jnp.int32, (rows, rows), 1
-    )
+    keys = jnp.concatenate(
+        [jnp.where(low, kv * scale, 0.0), jnp.where(low, 0.0, vk * scale)], axis=0
+    ).astype(BF16)
+    values = jnp.concatenate([jnp.where(low, vk, 0.0), jnp.where(low, 0.0, kv)], axis=0).astype(BF16)
+
+    def stacked(array):
+        return jnp.concatenate(
+            [array[:, p * lanes : (p + 1) * lanes] for p in range(q_width // lanes)], axis=0
+        )
+
+    query_st, d_attn_st = stacked(query), stacked(d_attn)
+    scores = dot(keys, query_st, NT)
+    d_share = dot(values, d_attn_st, NT)
+    width = scores.shape[1]
+    place = lax.broadcasted_iota(jnp.int32, (n_keys, width), 1) % rows + offset
+    causal = lax.broadcasted_iota(jnp.int32, (n_keys, width), 0) <= place
     shares, d_scores = [], []
-    for i in range(n_heads):
-        s = jnp.where(causal, scores[i * rows : (i + 1) * rows], -1e30)
+    for i in range(2):
+        s = jnp.where(causal, scores[i * n_keys : (i + 1) * n_keys], -1e30)
         e = jnp.exp(s - jnp.max(s, axis=0, keepdims=True))
         p = e / jnp.sum(e, axis=0, keepdims=True)
-        dp = d_share[i * rows : (i + 1) * rows]
+        dp = d_share[i * n_keys : (i + 1) * n_keys]
         ds = p * (dp - jnp.sum(p * dp, axis=0, keepdims=True))
         shares.append(p.astype(BF16))
         d_scores.append(ds.astype(BF16))
-    d_query = dot(jnp.concatenate(d_scores, axis=0), keys, TN)
-
-    def by_parity(blocks):
-        return jnp.concatenate(
-            [jnp.concatenate(blocks[0::2], axis=1), jnp.concatenate(blocks[1::2], axis=1)], axis=0
-        )
-
-    def stacked(array):
-        return jnp.concatenate(
-            [array[:, p * 2 * head : (p + 1) * 2 * head] for p in range(n_heads // 2)], axis=0
-        )
-
-    dk = dot(by_parity(d_scores), stacked(query), NN) * scale
-    dv = dot(by_parity(shares), stacked(d_attn), NN)
-    d_keyval = jnp.where(low, dk[:rows], dv[rows:]) + pltpu.roll(
-        jnp.where(low, dv[:rows], dk[rows:]), head, 1
+    shares = jnp.concatenate(shares, axis=0)
+    d_scores = jnp.concatenate(d_scores, axis=0)
+    d_query_st = dot(d_scores, keys, TN).astype(BF16)
+    d_query = jnp.concatenate(
+        [d_query_st[p * rows : (p + 1) * rows] for p in range(q_width // lanes)], axis=1
     )
-    return d_query.astype(BF16), d_keyval.astype(BF16)
+    dk = dot(d_scores, query_st, NN) * scale
+    dv = dot(shares, d_attn_st, NN)
+    d_keyval = jnp.where(low, dk[:n_keys], dv[n_keys:]) + pltpu.roll(
+        jnp.where(low, dv[:n_keys], dk[n_keys:]), head, 1
+    )
+    return d_query, d_keyval
+
+
+def folded(rows):
+    half = rows.shape[1] // 2
+    return jnp.concatenate([rows[:, :half], rows[:, half:]], axis=0)
+
+
+def unfolded(rows):
+    count = rows.shape[0] // 2
+    return jnp.concatenate([rows[:count], rows[count:]], axis=1)
 
 
 def kernel(
@@ -108,6 +104,11 @@
     landed,
     outs,
     final,
+    cot,
+    cot_folded,
+    xf_out,
+    xf,
+    carried,
     dkv,
     turned,
     core_out,
@@ -125,6 +126,8 @@
     rs_recv,
     fin_send,
     fin_recv,
+    xf_send,
+    xf_recv,
     core_send,
     core_recv,
     z1_send,
@@ -141,8 +144,11 @@
     n_z = n_dp // 2
     n_far = n_z // NEAR
     zi, zg = z % NEAR, z // NEAR
-    shard = outs.shape[1]
+    shard, half_width = outs.shape[2:]
+    small = shard // 2
     n_rows = q.shape[2]
+    half_rows = n_rows // 2
+    home = t // (n_tensor // 2)
     chunk = grad_ref.shape[1]
     first = s == 1
 
@@ -174,12 +180,13 @@
         pltpu.make_async_copy(src, dst, load_sem.at[i])
         for i, (src, dst) in enumerate(
             [
+                (cot_hbm, cot),
+                (xin_hbm, xin),
                 (wo_hbm, wo),
                 (q_hbm, q),
                 (kv_hbm, kv),
                 (wq_hbm, wq),
                 (wkv_hbm, wkv),
-                (xin_hbm, xin),
                 (gain_hbm, gain),
                 (xn_hbm, xn),
             ]
@@ -188,50 +195,125 @@
     for load in loads:
         load.start()
 
+    loads[0].wait()
+    for b in range(2):
+        cot_folded[b] = folded(cot[...].astype(F32)[b * small : (b + 1) * small]).astype(BF16)
+    loads[1].wait()
+    for i in range(4):
+        rows = xin[i // 2, i % 2].astype(F32)
+        for b in range(2):
+            xf_out[b, i] = folded(rows[b * small : (b + 1) * small]).astype(BF16)
+
     pl.semaphore_wait(barrier, 2 * n_tensor - 1 + 1 + NEAR - 1 + 2)
 
     def rows_of(index):
         return pl.ds(pl.multiple_of(index * shard, shard), shard)
 
-    def gather_copy(src, item, j, section):
-        return pltpu.make_async_remote_copy(
-            src_ref=src,
-            dst_ref=gathered.at[item, rows_of(t)],
-            send_sem=ag_send.at[item, j],
-            recv_sem=ag_recv.at[item, j],
+    def block_of(b):
+        return 2 * lax.rem(t, n_tensor // 2) + b
+
+    def start_copy(item, b, j, section):
+        return pltpu.make_async_remote_copy(
+            src_ref=cot_folded.at[b],
+            dst_ref=gathered.at[item, home, rows_of(block_of(b))],
+            send_sem=ag_send.at[b, j],
+            recv_sem=ag_recv.at[item, home, block_of(b)],
             device_id={"section": section, "tensor": tensor_peer(j)},
             device_id_type=MESH,
         )
 
-    def reply_copy(k, item, j):
-        return pltpu.make_async_remote_copy(
-            src_ref=outs.at[k],
-            dst_ref=gathered.at[item, rows_of(t)],
-            send_sem=out_send.at[k, j],
-            recv_sem=ag_recv.at[item, j],
+    def own_shard_copy(b):
+        return pltpu.make_async_copy(
+            cot_folded.at[b],
+            gathered.at[0, home, rows_of(block_of(b))],
+            ag_recv.at[0, home, block_of(b)],
+        )
+
+    def reply_copy(k, h, item, j):
+        return pltpu.make_async_remote_copy(
+            src_ref=outs.at[k, h],
+            dst_ref=gathered.at[item, h, rows_of(t)],
+            send_sem=out_send.at[k, h, j],
+            recv_sem=ag_recv.at[item, h, t],
             device_id={"section": 1 - s, "tensor": tensor_peer(j)},
             device_id_type=MESH,
         )
 
-    def own_shard_copy():
-        return pltpu.make_async_copy(cot_hbm, gathered.at[0, rows_of(t)], ag_recv.at[0, 0])
-
-    def reduce_copy(k, j):
-        return pltpu.make_async_remote_copy(
-            src_ref=parts.at[k, rows_of(tensor_peer(j))],
-            dst_ref=landed.at[k, rows_of(j)],
-            send_sem=rs_send.at[k, j],
-            recv_sem=rs_recv.at[k, j],
+    def arrival(k, h, r):
+        return pltpu.make_async_remote_copy(
+            src_ref=outs.at[0, h],
+            dst_ref=gathered.at[k, h, r * shard : (r + 1) * shard],
+            send_sem=out_send.at[0, h, 0],
+            recv_sem=ag_recv.at[k, h, r],
+            device_id={"section": 1 - s},
+            device_id_type=MESH,
+        )
+
+    def reduce_copy(k, h, j):
+        return pltpu.make_async_remote_copy(
+            src_ref=parts.at[k, h, rows_of(tensor_peer(j))],
+            dst_ref=landed.at[k, h, rows_of(j)],
+            send_sem=rs_send.at[k, h, j],
+            recv_sem=rs_recv.at[k, h, j],
             device_id={"tensor": tensor_peer(j)},
             device_id_type=MESH,
         )
 
-    def final_copy():
-        return pltpu.make_async_remote_copy(
-            src_ref=outs.at[2],
-            dst_ref=final,
-            send_sem=fin_send,
-            recv_sem=fin_recv,
+    def result_owner(h):
+        return h * (n_tensor // 2) + t // 2
+
+    def final_copy(k, h, section):
+        return pltpu.make_async_remote_copy(
+            src_ref=outs.at[k, h],
+            dst_ref=final.at[t % 2],
+            send_sem=fin_send.at[h],
+            recv_sem=fin_recv.at[t % 2],
+            device_id={"section": section, "tensor": result_owner(h)},
+            device_id_type=MESH,
+        )
+
+    def final_last(h):
+        return pltpu.make_async_remote_copy(
+            src_ref=outs.at[3, h],
+            dst_ref=final.at[t % 2],
+            send_sem=fin_send.at[2 + h],
+            recv_sem=fin_recv.at[t % 2],
+            device_id={"tensor": result_owner(h)},
+            device_id_type=MESH,
+        )
+
+    def final_own(k, h):
+        return pltpu.make_async_copy(outs.at[k, h], final.at[t % 2], fin_recv.at[t % 2])
+
+    def final_arrival(b):
+        return pltpu.make_async_remote_copy(
+            src_ref=outs.at[0, 0],
+            dst_ref=final.at[b],
+            send_sem=fin_send.at[0],
+            recv_sem=fin_recv.at[b],
+            device_id={"section": 1 - s},
+            device_id_type=MESH,
+        )
+
+    def input_copy(b):
+        return pltpu.make_async_remote_copy(
+            src_ref=xf_out.at[b],
+            dst_ref=xf.at[home],
+            send_sem=xf_send.at[b],
+            recv_sem=xf_recv.at[home],
+            device_id={"tensor": block_of(b)},
+            device_id_type=MESH,
+        )
+
+    def input_own(b):
+        return pltpu.make_async_copy(xf_out.at[b], xf.at[home], xf_recv.at[home])
+
+    def input_arrival(h):
+        return pltpu.make_async_remote_copy(
+            src_ref=xf_out.at[0],
+            dst_ref=xf.at[h],
+            send_sem=xf_send.at[0],
+            recv_sem=xf_recv.at[h],
             device_id={"section": 1 - s},
             device_id_type=MESH,
         )
@@ -352,56 +434,151 @@
 
     @pl.when(first)
     def _():
+        for b in range(2):
+            own_shard_copy(b).start()
         for j in range(1, n_tensor):
-            gather_copy(cot_hbm, 0, j, s).start()
-        own_shard_copy().start()
+            for b in range(2):
+                start_copy(0, b, j, s).start()
+
+    for b in range(2):
+
+        @pl.when(block_of(b) != t)
+        def _():
+            input_copy(b).start()
+
+        @pl.when(block_of(b) == t)
+        def _():
+            input_own(b).start()
 
     greet(0)
-    for load in loads:
+    for load in loads[2:]:
         load.wait()
+    turn(1)
 
     @pl.when(jnp.logical_not(first))
     def _():
         pl.semaphore_wait(go_sem, 1)
         for j in range(n_tensor):
-            gather_copy(cot_hbm, 1, j, 1 - s).start()
+            for b in range(2):
+                start_copy(1, b, j, 1 - s).start()
+
+    def norm_half(k, h, slot, micro):
+        x = xf[h, slot * 2 + micro].astype(F32)
+
+        def over_rows(values):
+            sums = jnp.sum(values, axis=-1, keepdims=True)
+            mean = (sums[:small] + sums[small:]) / (2 * half_width)
+            return jnp.concatenate([mean, mean], axis=0)
+
+        r = lax.rsqrt(over_rows(x * x) + 1e-05)
+        d_normed = parts[k, h, rows_of(t)].astype(F32)
+        for j in range(1, n_tensor):
+            reduce_copy(k, h, j).wait_recv()
+            d_normed = d_normed + landed[k, h, j * shard : (j + 1) * shard].astype(F32)
+        row = gain[slot]
+        gains = jnp.concatenate(
+            [
+                jnp.broadcast_to(row[:, :half_width], (small, half_width)),
+                jnp.broadcast_to(row[:, half_width:], (small, half_width)),
+            ],
+            axis=0,
+        )
+        scaled = d_normed * gains
+        d_input = r * scaled - x * (r * r * r * over_rows(x * scaled))
+        outs[k, h] = (gathered[k, h, rows_of(t)].astype(F32) + d_input).astype(BF16)
+
+        @pl.when(first)
+        def _():
+            for j in range(n_tensor):
+                reply_copy(k, h, k, j).start()
+
+        @pl.when(jnp.logical_and(jnp.logical_not(first), k < 2))
+        def _():
+            for j in range(n_tensor):
+                reply_copy(k, h, k + 2, j).start()
+
+        @pl.when(jnp.logical_and(jnp.logical_not(first), k == 2))
+        def _():
+            final_copy(k, h, 1 - s).start()
+
+        @pl.when(jnp.logical_and(jnp.logical_not(first), k == 3))
+        def _():
+            @pl.when(result_owner(h) != t)
+            def _():
+                final_last(h).start()
+
+            @pl.when(result_owner(h) == t)
+            def _():
+                final_own(k, h).start()
 
     def step(k, carry):
         slot = 1 - k // 2
         place = k % 2
         micro = 1 - place
         tail = jnp.logical_and(k == 3, jnp.logical_not(first))
-        for j in range(n_tensor):
-            gather_copy(outs.at[0], k, j, s).wait_recv()
+        for h in (1, 0):
+            for r in range(n_tensor):
+                arrival(k, h, r).wait_recv()
+            low = dot(gathered[k, h], wo[slot, :, :half_width], NT)
+            high = dot(gathered[k, h], wo[slot, :, half_width:], NT)
+            d_attn = jnp.concatenate(
+                [
+                    low[r * shard : r * shard + small] + high[r * shard + small : (r + 1) * shard]
+                    for r in range(n_tensor)
+                ],
+                axis=0,
+            ).astype(BF16)
+            base = h * half_rows
+            d_query, d_keyval = attention_grads(
+                q[slot, micro, base : base + half_rows],
+                kv[slot, micro, : base + half_rows],
+                d_attn,
+                base,
+            )
+            if h:
+                carried[...] = d_keyval[:half_rows]
+                d_keyval = d_keyval[half_rows:].astype(BF16)
+            else:
+                d_keyval = (d_keyval + carried[...]).astype(BF16)
+            dkv[slot, pl.ds(pl.multiple_of(place * n_rows + base, half_rows), half_rows)] = d_keyval
+
+            if not h:
+
+                @pl.when(tail)
+                def _():
+                    gradient(0)
+
+            tile = half_width // 2
+            for c in range(2):
+                sides = []
+                for side in range(2):
+                    span = slice(side * half_width + c * tile, side * half_width + (c + 1) * tile)
+                    sides.append(
+                        dot(d_query, wq[slot, span], NT) + dot(d_keyval, wkv[slot, span], NT)
+                    )
+                blocks = []
+                for r in range(n_tensor):
+                    blocks += [side[r * small : (r + 1) * small] for side in sides]
+                parts[k, h, :, c * tile : (c + 1) * tile] = jnp.concatenate(blocks, axis=0).astype(BF16)
+            for j in range(1, n_tensor):
+                reduce_copy(k, h, j).start()
 
         @pl.when(jnp.logical_and(first, k == 0))
         def _():
             pl.semaphore_signal(go_sem, inc=1, device_id={"section": 1 - s}, device_id_type=MESH)
 
-        d_attn = dot(gathered[k], wo[slot], NT).astype(BF16)
-        d_query, d_keyval = attention_grads(q[slot, micro], kv[slot, micro], d_attn)
-        dkv[slot, pl.ds(pl.multiple_of(place * n_rows, n_rows), n_rows)] = d_keyval
-
-        @pl.when(tail)
-        def _():
-            gradient(0)
-
-        parts[k] = (dot(d_query, wq[slot], NT) + dot(d_keyval, wkv[slot], NT)).astype(BF16)
-
-        @pl.when(tail)
-        def _():
-            near_phase(0)
-
-        for j in range(1, n_tensor):
-            reduce_copy(k, j).start()
-
-        @pl.when(place == 0)
-        def _():
-            turn(slot)
+        @pl.when(k == 0)
+        def _():
+            turn(0)
+            for h in range(2):
+                input_arrival(h).wait_recv()
 
         @pl.when(jnp.logical_and(place == 1, jnp.logical_not(tail)))
         def _():
             gradient(slot)
+
+        @pl.when(place == 1)
+        def _():
             near_phase(slot)
 
         @pl.when(k < 2)
@@ -414,66 +591,56 @@
             greeted(2)
             far_phase(1)
 
-        @pl.when(tail)
-        def _():
-            far_phase(0)
-
-        x = xin[slot, micro].astype(F32)
-        mean_sq = jnp.mean(x * x, axis=-1, keepdims=True)
-        r = lax.rsqrt(mean_sq + 1e-05)
-        d_normed = parts[k, rows_of(t)].astype(F32)
-        for j in range(1, n_tensor):
-            reduce_copy(k, j).wait_recv()
-            d_normed = d_normed + landed[k, j * shard : (j + 1) * shard].astype(F32)
-        scaled = d_normed * gain[slot]
-        along = jnp.mean(x * scaled, axis=-1, keepdims=True)
-        d_input = r * scaled - x * (r * r * r * along)
-        outs[k] = (gathered[k, rows_of(t)].astype(F32) + d_input).astype(BF16)
-
-        @pl.when(first)
-        def _():
-            for j in range(n_tensor):
-                reply_copy(k, k, j).start()
-
-        @pl.when(jnp.logical_and(jnp.logical_not(first), k < 2))
-        def _():
-            for j in range(n_tensor):
-                reply_copy(k, k + 2, j).start()
-
-        @pl.when(jnp.logical_and(jnp.logical_not(first), k == 2))
-        def _():
-            final_copy().start()
-
+        for h in (1, 0):
+            norm_half(k, h, slot, micro)
         return carry
 
     lax.fori_loop(0, 4, step, 0)
+    far_phase(0)
+    for b in range(2):
+        final_arrival(b).wait_recv()
+    out_ref[...] = jnp.concatenate(
+        [unfolded(final[b].astype(F32)) for b in range(2)], axis=0
+    ).astype(BF16)
 
     @pl.when(first)
     def _():
-        far_phase(0)
-        final_copy().wait_recv()
-        out_ref[...] = final[...]
         for j in range(1, n_tensor):
-            gather_copy(cot_hbm, 0, j, s).wait_send()
+            for b in range(2):
+                start_copy(0, b, j, s).wait_send()
         for k in range(4):
-            for j in range(n_tensor):
-                reply_copy(k, k, j).wait_send()
+            for h in range(2):
+                for j in range(n_tensor):
+                    reply_copy(k, h, k, j).wait_send()
 
     @pl.when(jnp.logical_not(first))
     def _():
-        out_ref[...] = outs[3]
-        final_copy().wait_send()
         for j in range(n_tensor):
-            gather_copy(cot_hbm, 1, j, 1 - s).wait_send()
+            for b in range(2):
+                start_copy(1, b, j, 1 - s).wait_send()
         for k in range(2):
-            for j in range(n_tensor):
-                reply_copy(k, k + 2, j).wait_send()
+            for h in range(2):
+                for j in range(n_tensor):
+                    reply_copy(k, h, k + 2, j).wait_send()
+        for h in range(2):
+            final_copy(2, h, 1 - s).wait_send()
+
+            @pl.when(result_owner(h) != t)
+            def _():
+                final_last(h).wait_send()
+
+    for b in range(2):
+
+        @pl.when(block_of(b) != t)
+        def _():
+            input_copy(b).wait_send()
 
     last_phase(1)
     last_phase(0)
     for k in range(4):
-        for j in range(1, n_tensor):
-            reduce_copy(k, j).wait_send()
+        for h in range(2):
+            for j in range(1, n_tensor):
+                reduce_copy(k, h, j).wait_send()
     for slot in range(2):
         core_copy(slot).wait_send()
         for j in range(1, NEAR):
@@ -522,11 +689,16 @@
             pltpu.VMEM((layers, width, q_width), BF16),
             pltpu.VMEM((layers, width, kv_width), BF16),
             pltpu.VMEM((layers, q_width, width), BF16),
-            pltpu.VMEM((items, n_rows, width), BF16),
-            pltpu.VMEM((items, n_rows, width), BF16),
-            pltpu.VMEM((items, n_rows, width), BF16),
-            pltpu.VMEM((items, shard, width), BF16),
+            pltpu.VMEM((items, 2, n_rows, width // 2), BF16),
+            pltpu.VMEM((items, 2, n_rows, width // 2), BF16),
+            pltpu.VMEM((items, 2, n_rows, width // 2), BF16),
+            pltpu.VMEM((items, 2, shard, width // 2), BF16),
+            pltpu.VMEM((2, shard, width // 2), BF16),
             pltpu.VMEM((shard, width), BF16),
+            pltpu.VMEM((2, shard, width // 2), BF16),
+            pltpu.VMEM((2, items, shard, width // 2), BF16),
+            pltpu.VMEM((2, items, shard, width // 2), BF16),
+            pltpu.VMEM((n_rows // 2, kv_width), F32),
             pltpu.VMEM((layers, micros * n_rows, kv_width), BF16),
             pltpu.VMEM((layers, 2, width // 2, micros * n_rows), BF16),
             pltpu.VMEM((layers, width // 2, kv_width), BF16),
@@ -536,14 +708,16 @@
             pltpu.VMEM((layers, NEAR, n_far * chunk, kv_width), BF16),
             pltpu.VMEM((layers, n_far, chunk, kv_width), BF16),
             pltpu.VMEM((layers, n_far, chunk, kv_width), BF16),
-            dma((8,)),
-            dma((items, n_tensor)),
-            dma((items, n_tensor)),
-            dma((items, n_tensor)),
-            dma((items, n_tensor)),
-            dma((items, n_tensor)),
-            dma(()),
-            dma(()),
+            dma((9,)),
+            dma((2, n_tensor)),
+            dma((items, 2, n_tensor)),
+            dma((items, 2, n_tensor)),
+            dma((items, 2, n_tensor)),
+            dma((items, 2, n_tensor)),
+            dma((4,)),
+            dma((2,)),
+            dma((2,)),
+            dma((2,)),
             dma((layers,)),
             dma((layers,)),
             dma((layers, NEAR)),

time: 138 us -> 127 us (0.920)
  the two profiles are of different devices: /device:TPU:96 before, /device:TPU:100 now
where the time goes in v2:
time: 127 us
  Pallas kernels  123 us (97%)
  local copies, waits for them, and re-layouts  2.85 us (2%)
    pallas_call x1, Pallas kernels, on_device(): pl.pallas_call(functools.partial(kernel, n_tensor, n_dp), out_shape=(jax....  123 us
    unnamed x2, local copies, waits for them, and re-layouts  2.85 us

profile of v2, /device:TPU:100, one launch (start us, length us, event | category | flops | bytes accessed | tf_op | source)
XLA Modules:
  0.0 126.6 jit_solution(8441869733951769938)
XLA Ops:
  0.6 123.1 %backward.1 = (bf16[16,2048]{1,0:T(8,128)(2,1)}, f32[2,32,128]{2,1,0:T(8,128)}) custom-call(bf16[16,2048]{1,0:T(8,128)(2,1)} %bitcast.19, bf16[2,2,16,2048]{3,2,1,0:T(8,128)(2,1)} %bitcast.16, bf16[2,2,128,2048]{3,2,1,0:T(8,128)(2,1)} %bitcast.12, bf16[2,2,128,256]{3,2,1,0:T(8,128)(2,1)} %bitcast.17, bf16[2,2,128,128]{3,2,1,0:T(8,128)(2,1)} %bitcast.18, ...), custom_call_target="tpu_custom_call" | custom-call | tf_op jit(solution)/shard_map/backward/pallas_call | solution.py:675
  123.7 1.5 %copy.14 = bf16[1,1,16,2048]{3,2,1,0:T(8,128)(2,1)} copy(bf16[1,1,16,2048]{3,2,1,0:T(8,128)(2,1)} %bitcast.20) | data formatting | bytes 131072
  125.2 1.4 %copy.15 = f32[2,1,32,1,128]{4,3,2,1,0:T(1,128)} copy(f32[2,1,32,1,128]{4,3,2,1,0:T(1,128)} %bitcast.21) | data formatting | bytes 65536

commit v3 on v2

--- a/solution.py
+++ b/solution.py
@@ -109,6 +109,7 @@
     xf_out,
     xf,
     carried,
+    kept,
     dkv,
     turned,
     core_out,
@@ -152,8 +153,17 @@
     chunk = grad_ref.shape[1]
     first = s == 1
 
+    n_x = n_tensor // 2
+    ty, tx = t // n_x, lax.rem(t, n_x)
+
     def tensor_peer(j):
-        return lax.rem(t + j, n_tensor)
+        return lax.rem(ty + j // n_x, 2) * n_x + lax.rem(tx + j % n_x, n_x)
+
+    def distance(j):
+        return 2 * (j // n_x) + min(j % n_x, n_x - j % n_x)
+
+    others = sorted(range(1, n_tensor), key=lambda j: -distance(j))
+    everyone = sorted(range(n_tensor), key=lambda j: -min(j % n_x, n_x - j % n_x))
 
     def near_peer(j):
         return (zg * NEAR + lax.rem(zi + j, NEAR)) * 2 + core
@@ -328,19 +338,20 @@
             device_id_type=MESH,
         )
 
-    def near_copy(slot, j):
-        return pltpu.make_async_remote_copy(
-            src_ref=z1_out.at[slot, lax.rem(zi + j, NEAR)],
-            dst_ref=z1_in.at[slot, j],
-            send_sem=z1_send.at[slot, j],
-            recv_sem=z1_recv.at[slot, j],
+    def near_copy(slot, part, j):
+        span = pl.ds(part * (n_far // 2), n_far // 2)
+        return pltpu.make_async_remote_copy(
+            src_ref=z1_out.at[slot, lax.rem(zi + j, NEAR), span],
+            dst_ref=z1_in.at[slot, j, span],
+            send_sem=z1_send.at[slot, part, j],
+            recv_sem=z1_recv.at[slot, part, j],
             device_id={"dp": near_peer(j)},
             device_id_type=MESH,
         )
 
     def far_copy(slot, j):
         return pltpu.make_async_remote_copy(
-            src_ref=z2_out.at[slot, lax.rem(zg + j, n_far)],
+            src_ref=z2_out.at[slot, j],
             dst_ref=z2_in.at[slot, j],
             send_sem=z2_send.at[slot, j],
             recv_sem=z2_recv.at[slot, j],
@@ -397,33 +408,38 @@
         core_copy(slot).start()
         lax.fori_loop(0, count, ours, 0)
 
+    far_order = [(i + n_far // 4) % n_far for i in range(n_far)]
+
+    def sum_rows(i, j):
+        where = (i * n_far + lax.rem(zg + j, n_far)) * chunk
+        return pl.ds(pl.multiple_of(where, chunk), chunk)
+
     def near_phase(slot):
         core_copy(slot).wait_recv()
-        block = n_far * chunk
-        for i in range(NEAR):
-            span = slice(i * block, (i + 1) * block)
-            total = core_own[slot, span] + core_in[slot, span].astype(F32)
-            core_own[slot, span] = total
-            z1_out[slot, i] = total.astype(BF16)
+        for part in range(2):
+            for i in range(NEAR):
+                for place in range(part * (n_far // 2), (part + 1) * (n_far // 2)):
+                    span = sum_rows(i, far_order[place])
+                    total = core_own[slot, span] + core_in[slot, span].astype(F32)
+                    core_own[slot, span] = total
+                    z1_out[slot, i, place] = total.astype(BF16)
+            for j in range(1, NEAR):
+                near_copy(slot, part, j).start()
+
+    def far_phase(slot, part):
         for j in range(1, NEAR):
-            near_copy(slot, j).start()
-
-    def far_phase(slot):
-        block = n_far * chunk
-        total = core_own[slot, pl.ds(pl.multiple_of(zi * block, block), block)]
-        for j in range(1, NEAR):
-            near_copy(slot, j).wait_recv()
-            total = total + z1_in[slot, j].astype(F32)
-        for g in range(n_far):
-            piece = total[g * chunk : (g + 1) * chunk]
-            z2_out[slot, g] = piece.astype(BF16)
-
-            @pl.when(g == zg)
-            def _():
-                grad_ref[slot] = piece
-
-        for j in range(1, n_far):
-            far_copy(slot, j).start()
+            near_copy(slot, part, j).wait_recv()
+        places = range(part * (n_far // 2), (part + 1) * (n_far // 2))
+        for place in sorted(places, key=lambda p: abs(far_order[p] - n_far // 2)):
+            j = far_order[place]
+            total = core_own[slot, sum_rows(zi, j)]
+            for i in range(1, NEAR):
+                total = total + z1_in[slot, i, place].astype(F32)
+            if j:
+                z2_out[slot, j] = total.astype(BF16)
+                far_copy(slot, j).start()
+            else:
+                grad_ref[slot] = total
 
     def last_phase(slot):
         total = grad_ref[slot]
@@ -436,7 +452,7 @@
     def _():
         for b in range(2):
             own_shard_copy(b).start()
-        for j in range(1, n_tensor):
+        for j in others:
             for b in range(2):
                 start_copy(0, b, j, s).start()
 
@@ -489,12 +505,12 @@
 
         @pl.when(first)
         def _():
-            for j in range(n_tensor):
+            for j in everyone:
                 reply_copy(k, h, k, j).start()
 
         @pl.when(jnp.logical_and(jnp.logical_not(first), k < 2))
         def _():
-            for j in range(n_tensor):
+            for j in everyone:
                 reply_copy(k, h, k + 2, j).start()
 
         @pl.when(jnp.logical_and(jnp.logical_not(first), k == 2))
@@ -510,6 +526,27 @@
             @pl.when(result_owner(h) == t)
             def _():
                 final_own(k, h).start()
+
+    def kv_rows(h, place):
+        start = place * n_rows + h * half_rows
+        return pl.ds(pl.multiple_of(start, half_rows), half_rows)
+
+    def project(k, h, slot, place):
+        d_query, d_keyval = kept[h], dkv[slot, kv_rows(h, place)]
+        tile = half_width // 2
+        for c in range(2):
+            sides = []
+            for side in range(2):
+                span = slice(side * half_width + c * tile, side * half_width + (c + 1) * tile)
+                sides.append(dot(d_query, wq[slot, span], NT) + dot(d_keyval, wkv[slot, span], NT))
+            blocks = []
+            for r in range(n_tensor):
+                blocks += [side[r * small : (r + 1) * small] for side in sides]
+            parts[k, h, :, c * tile : (c + 1) * tile] = jnp.concatenate(blocks, axis=0).astype(BF16)
+
+    def scatter(k, h):
+        for j in others:
+            reduce_copy(k, h, j).start()
 
     def step(k, carry):
         slot = 1 - k // 2
@@ -540,28 +577,30 @@
                 d_keyval = d_keyval[half_rows:].astype(BF16)
             else:
                 d_keyval = (d_keyval + carried[...]).astype(BF16)
-            dkv[slot, pl.ds(pl.multiple_of(place * n_rows + base, half_rows), half_rows)] = d_keyval
-
-            if not h:
+            dkv[slot, kv_rows(h, place)] = d_keyval
+            kept[h] = d_query
+            if h:
+
+                @pl.when(jnp.logical_not(tail))
+                def _():
+                    project(k, 1, slot, place)
+                    scatter(k, 1)
+
+            else:
 
                 @pl.when(tail)
                 def _():
                     gradient(0)
-
-            tile = half_width // 2
-            for c in range(2):
-                sides = []
-                for side in range(2):
-                    span = slice(side * half_width + c * tile, side * half_width + (c + 1) * tile)
-                    sides.append(
-                        dot(d_query, wq[slot, span], NT) + dot(d_keyval, wkv[slot, span], NT)
-                    )
-                blocks = []
-                for r in range(n_tensor):
-                    blocks += [side[r * small : (r + 1) * small] for side in sides]
-                parts[k, h, :, c * tile : (c + 1) * tile] = jnp.concatenate(blocks, axis=0).astype(BF16)
-            for j in range(1, n_tensor):
-                reduce_copy(k, h, j).start()
+                    project(k, 1, slot, place)
+                    scatter(k, 1)
+
+                project(k, 0, slot, place)
+
+                @pl.when(tail)
+                def _():
+                    near_phase(0)
+
+                scatter(k, 0)
 
         @pl.when(jnp.logical_and(first, k == 0))
         def _():
@@ -577,26 +616,42 @@
         def _():
             gradient(slot)
 
-        @pl.when(place == 1)
-        def _():
-            near_phase(slot)
-
         @pl.when(k < 2)
         def _():
             greeted(k)
             greet(k + 1)
 
+        @pl.when(tail)
+        def _():
+            far_phase(0, 0)
+
+        norm_half(k, 1, slot, micro)
+
+        @pl.when(tail)
+        def _():
+            far_phase(0, 1)
+
+        norm_half(k, 0, slot, micro)
+
+        @pl.when(jnp.logical_and(place == 1, jnp.logical_not(tail)))
+        def _():
+            near_phase(slot)
+
         @pl.when(k == 2)
         def _():
             greeted(2)
-            far_phase(1)
-
-        for h in (1, 0):
-            norm_half(k, h, slot, micro)
+            far_phase(1, 0)
+            far_phase(1, 1)
+
         return carry
 
     lax.fori_loop(0, 4, step, 0)
-    far_phase(0)
+
+    @pl.when(first)
+    def _():
+        far_phase(0, 0)
+        far_phase(0, 1)
+
     for b in range(2):
         final_arrival(b).wait_recv()
     out_ref[...] = jnp.concatenate(
@@ -643,10 +698,22 @@
                 reduce_copy(k, h, j).wait_send()
     for slot in range(2):
         core_copy(slot).wait_send()
-        for j in range(1, NEAR):
-            near_copy(slot, j).wait_send()
+        for part in range(2):
+            for j in range(1, NEAR):
+                near_copy(slot, part, j).wait_send()
         for j in range(1, n_far):
             far_copy(slot, j).wait_send()
+
+
+def handed_on(rows_ref, grad_ref, rows_out, grad_out, sems):
+    copies = [
+        pltpu.make_async_copy(rows_ref, rows_out, sems.at[0]),
+        pltpu.make_async_copy(grad_ref, grad_out, sems.at[1]),
+    ]
+    for copy in copies:
+        copy.start()
+    for copy in copies:
+        copy.wait()
 
 
 def on_device(
@@ -699,13 +766,14 @@
             pltpu.VMEM((2, items, shard, width // 2), BF16),
             pltpu.VMEM((2, items, shard, width // 2), BF16),
             pltpu.VMEM((n_rows // 2, kv_width), F32),
+            pltpu.VMEM((2, n_rows // 2, q_width), BF16),
             pltpu.VMEM((layers, micros * n_rows, kv_width), BF16),
             pltpu.VMEM((layers, 2, width // 2, micros * n_rows), BF16),
             pltpu.VMEM((layers, width // 2, kv_width), BF16),
             pltpu.VMEM((layers, width // 2, kv_width), F32),
             pltpu.VMEM((layers, width // 2, kv_width), BF16),
-            pltpu.VMEM((layers, NEAR, n_far * chunk, kv_width), BF16),
-            pltpu.VMEM((layers, NEAR, n_far * chunk, kv_width), BF16),
+            pltpu.VMEM((layers, NEAR, n_far, chunk, kv_width), BF16),
+            pltpu.VMEM((layers, NEAR, n_far, chunk, kv_width), BF16),
             pltpu.VMEM((layers, n_far, chunk, kv_width), BF16),
             pltpu.VMEM((layers, n_far, chunk, kv_width), BF16),
             dma((9,)),
@@ -720,8 +788,8 @@
             dma((2,)),
             dma((layers,)),
             dma((layers,)),
-            dma((layers, NEAR)),
-            dma((layers, NEAR)),
+            dma((layers, 2, NEAR)),
+            dma((layers, 2, NEAR)),
             dma((layers, n_far)),
             dma((layers, n_far)),
             pltpu.SemaphoreType.REGULAR,
@@ -742,6 +810,17 @@
         w_keyval.reshape(layers, width, kv_width),
         w_output.reshape(layers, q_width, width),
     )
+    input_grad, keyval_grad = pl.pallas_call(
+        handed_on,
+        out_shape=(
+            jax.ShapeDtypeStruct(input_grad.shape, BF16),
+            jax.ShapeDtypeStruct(keyval_grad.shape, F32),
+        ),
+        in_specs=[any_spec] * 2,
+        out_specs=(any_spec, any_spec),
+        scratch_shapes=[dma((2,))],
+        name="results",
+    )(input_grad, keyval_grad)
     return (
         input_grad[None, None],
         keyval_grad.reshape(layers, 1, chunk, 1, kv_width),

time: 127 us -> 128 us (level)
  the two profiles are of different devices: /device:TPU:100 before, /device:TPU:96 now
where the time goes in v3:
time: 128 us
  Pallas kernels  127 us (99%)
    pallas_call x1, Pallas kernels, on_device(): pl.pallas_call(functools.partial(kernel, n_tensor, n_dp), out_shape=(jax....  123 us
    pallas_call x1, Pallas kernels, on_device(): pl.pallas_call(handed_on, out_shape=(jax.ShapeDtypeStruct(input_grad.shap...  4.1 us

profile of v3, /device:TPU:96, one launch (start us, length us, event | category | flops | bytes accessed | tf_op | source)
XLA Modules:
  0.0 128.1 jit_solution(12543321751846389000)
XLA Ops:
  0.6 123.4 %backward.1 = (bf16[16,2048]{1,0:T(8,128)(2,1)}, f32[2,32,128]{2,1,0:T(8,128)}) custom-call(bf16[16,2048]{1,0:T(8,128)(2,1)} %bitcast.19, bf16[2,2,16,2048]{3,2,1,0:T(8,128)(2,1)} %bitcast.16, bf16[2,2,128,2048]{3,2,1,0:T(8,128)(2,1)} %bitcast.12, bf16[2,2,128,256]{3,2,1,0:T(8,128)(2,1)} %bitcast.17, bf16[2,2,128,128]{3,2,1,0:T(8,128)(2,1)} %bitcast.18, ...), custom_call_target="tpu_custom_call" | custom-call | tf_op jit(solution)/shard_map/backward/pallas_call | solution.py:742
  124.0 4.1 %results.1 = (bf16[16,2048]{1,0:T(8,128)(2,1)}, f32[2,32,128]{2,1,0:T(8,128)}) custom-call(bf16[16,2048]{1,0:T(8,128)(2,1)} %get-tuple-element.6.rows_ref, f32[2,32,128]{2,1,0:T(8,128)} %get-tuple-element.7.grad_ref), custom_call_target="tpu_custom_call" | custom-call | tf_op jit(solution)/shard_map/results/pallas_call | solution.py:813

commit v4 on v3

--- a/solution.py
+++ b/solution.py
@@ -163,7 +163,6 @@
         return 2 * (j // n_x) + min(j % n_x, n_x - j % n_x)
 
     others = sorted(range(1, n_tensor), key=lambda j: -distance(j))
-    everyone = sorted(range(n_tensor), key=lambda j: -min(j % n_x, n_x - j % n_x))
 
     def near_peer(j):
         return (zg * NEAR + lax.rem(zi + j, NEAR)) * 2 + core
@@ -245,7 +244,7 @@
             dst_ref=gathered.at[item, h, rows_of(t)],
             send_sem=out_send.at[k, h, j],
             recv_sem=ag_recv.at[item, h, t],
-            device_id={"section": 1 - s, "tensor": tensor_peer(j)},
+            device_id={"section": 1 - s, "tensor": lax.rem(t + j, n_tensor)},
             device_id_type=MESH,
         )
 
@@ -505,12 +504,12 @@
 
         @pl.when(first)
         def _():
-            for j in everyone:
+            for j in range(n_tensor):
                 reply_copy(k, h, k, j).start()
 
         @pl.when(jnp.logical_and(jnp.logical_not(first), k < 2))
         def _():
-            for j in everyone:
+            for j in range(n_tensor):
                 reply_copy(k, h, k + 2, j).start()
 
         @pl.when(jnp.logical_and(jnp.logical_not(first), k == 2))
@@ -703,17 +702,6 @@
                 near_copy(slot, part, j).wait_send()
         for j in range(1, n_far):
             far_copy(slot, j).wait_send()
-
-
-def handed_on(rows_ref, grad_ref, rows_out, grad_out, sems):
-    copies = [
-        pltpu.make_async_copy(rows_ref, rows_out, sems.at[0]),
-        pltpu.make_async_copy(grad_ref, grad_out, sems.at[1]),
-    ]
-    for copy in copies:
-        copy.start()
-    for copy in copies:
-        copy.wait()
 
 
 def on_device(
@@ -810,17 +798,6 @@
         w_keyval.reshape(layers, width, kv_width),
         w_output.reshape(layers, q_width, width),
     )
-    input_grad, keyval_grad = pl.pallas_call(
-        handed_on,
-        out_shape=(
-            jax.ShapeDtypeStruct(input_grad.shape, BF16),
-            jax.ShapeDtypeStruct(keyval_grad.shape, F32),
-        ),
-        in_specs=[any_spec] * 2,
-        out_specs=(any_spec, any_spec),
-        scratch_shapes=[dma((2,))],
-        name="results",
-    )(input_grad, keyval_grad)
     return (
         input_grad[None, None],
         keyval_grad.reshape(layers, 1, chunk, 1, kv_width),

time: 128 us -> 127 us (level)
  the two profiles are of different devices: /device:TPU:96 before, /device:TPU:4 now
where the time goes in v4:
time: 127 us
  Pallas kernels  124 us (98%)
  local copies, waits for them, and re-layouts  2.85 us (2%)
    pallas_call x1, Pallas kernels, on_device(): pl.pallas_call(functools.partial(kernel, n_tensor, n_dp), out_shape=(jax....  124 us
    unnamed x2, local copies, waits for them, and re-layouts  2.85 us

profile of v4, /device:TPU:4, one launch (start us, length us, event | category | flops | bytes accessed | tf_op | source)
XLA Modules:
  0.0 127.1 jit_solution(800124142241740421)
XLA Ops:
  0.6 123.6 %backward.1 = (bf16[16,2048]{1,0:T(8,128)(2,1)}, f32[2,32,128]{2,1,0:T(8,128)}) custom-call(bf16[16,2048]{1,0:T(8,128)(2,1)} %bitcast.19, bf16[2,2,16,2048]{3,2,1,0:T(8,128)(2,1)} %bitcast.16, bf16[2,2,128,2048]{3,2,1,0:T(8,128)(2,1)} %bitcast.12, bf16[2,2,128,256]{3,2,1,0:T(8,128)(2,1)} %bitcast.17, bf16[2,2,128,128]{3,2,1,0:T(8,128)(2,1)} %bitcast.18, ...), custom_call_target="tpu_custom_call" | custom-call | tf_op jit(solution)/shard_map/backward/pallas_call | solution.py:730
  124.2 1.5 %copy.14 = bf16[1,1,16,2048]{3,2,1,0:T(8,128)(2,1)} copy(bf16[1,1,16,2048]{3,2,1,0:T(8,128)(2,1)} %bitcast.20) | data formatting | bytes 131072
  125.7 1.4 %copy.15 = f32[2,1,32,1,128]{4,3,2,1,0:T(1,128)} copy(f32[2,1,32,1,128]{4,3,2,1,0:T(1,128)} %bitcast.21) | data formatting | bytes 65536

commit v5 on v4

--- a/solution.py
+++ b/solution.py
@@ -20,47 +20,60 @@
     return lax.dot_general(a, b, dims, preferred_element_type=F32)
 
 
-def attention_grads(query, keyval, d_attn, offset):
-    rows, q_width = query.shape
+def padded(keyval):
     n_keys, lanes = keyval.shape
     head = lanes // 2
-    scale = head**-0.5
     low = lax.broadcasted_iota(jnp.int32, (n_keys, lanes), 1) < head
     kv = keyval.astype(F32)
     vk = pltpu.roll(kv, head, 1)
     keys = jnp.concatenate(
-        [jnp.where(low, kv * scale, 0.0), jnp.where(low, 0.0, vk * scale)], axis=0
+        [jnp.where(low, kv * head**-0.5, 0.0), jnp.where(low, 0.0, vk * head**-0.5)], axis=0
     ).astype(BF16)
     values = jnp.concatenate([jnp.where(low, vk, 0.0), jnp.where(low, 0.0, kv)], axis=0).astype(BF16)
-
-    def stacked(array):
-        return jnp.concatenate(
-            [array[:, p * lanes : (p + 1) * lanes] for p in range(q_width // lanes)], axis=0
-        )
-
-    query_st, d_attn_st = stacked(query), stacked(d_attn)
-    scores = dot(keys, query_st, NT)
-    d_share = dot(values, d_attn_st, NT)
+    return keys, values, low
+
+
+def stacked(array, lanes):
+    return jnp.concatenate(
+        [array[:, p * lanes : (p + 1) * lanes] for p in range(array.shape[1] // lanes)], axis=0
+    )
+
+
+def attention_shares(query, keyval, offset):
+    rows = query.shape[0]
+    n_keys, lanes = keyval.shape
+    keys, _, _ = padded(keyval)
+    scores = dot(keys, stacked(query, lanes), NT)
     width = scores.shape[1]
     place = lax.broadcasted_iota(jnp.int32, (n_keys, width), 1) % rows + offset
     causal = lax.broadcasted_iota(jnp.int32, (n_keys, width), 0) <= place
-    shares, d_scores = [], []
+    shares = []
     for i in range(2):
         s = jnp.where(causal, scores[i * n_keys : (i + 1) * n_keys], -1e30)
         e = jnp.exp(s - jnp.max(s, axis=0, keepdims=True))
-        p = e / jnp.sum(e, axis=0, keepdims=True)
+        shares.append(e / jnp.sum(e, axis=0, keepdims=True))
+    return jnp.concatenate(shares, axis=0)
+
+
+def attention_grads(query, keyval, d_attn, shares):
+    rows, q_width = query.shape
+    n_keys, lanes = keyval.shape
+    head = lanes // 2
+    keys, values, low = padded(keyval)
+    query_st, d_attn_st = stacked(query, lanes), stacked(d_attn, lanes)
+    d_share = dot(values, d_attn_st, NT)
+    d_scores = []
+    for i in range(2):
+        p = shares[i * n_keys : (i + 1) * n_keys]
         dp = d_share[i * n_keys : (i + 1) * n_keys]
-        ds = p * (dp - jnp.sum(p * dp, axis=0, keepdims=True))
-        shares.append(p.astype(BF16))
-        d_scores.append(ds.astype(BF16))
-    shares = jnp.concatenate(shares, axis=0)
+        d_scores.append((p * (dp - jnp.sum(p * dp, axis=0, keepdims=True))).astype(BF16))
     d_scores = jnp.concatenate(d_scores, axis=0)
     d_query_st = dot(d_scores, keys, TN).astype(BF16)
     d_query = jnp.concatenate(
         [d_query_st[p * rows : (p + 1) * rows] for p in range(q_width // lanes)], axis=1
     )
-    dk = dot(d_scores, query_st, NN) * scale
-    dv = dot(shares, d_attn_st, NN)
+    dk = dot(d_scores, query_st, NN) * head**-0.5
+    dv = dot(shares.astype(BF16), d_attn_st, NN)
     d_keyval = jnp.where(low, dk[:n_keys], dv[n_keys:]) + pltpu.roll(
         jnp.where(low, dv[:n_keys], dk[n_keys:]), head, 1
     )
@@ -110,6 +123,7 @@
     xf,
     carried,
     kept,
+    shares,
     dkv,
     turned,
     core_out,
@@ -258,12 +272,13 @@
             device_id_type=MESH,
         )
 
-    def reduce_copy(k, h, j):
-        return pltpu.make_async_remote_copy(
-            src_ref=parts.at[k, h, rows_of(tensor_peer(j))],
-            dst_ref=landed.at[k, h, rows_of(j)],
-            send_sem=rs_send.at[k, h, j],
-            recv_sem=rs_recv.at[k, h, j],
+    def reduce_copy(k, h, c, j):
+        span = pl.ds(c * (half_width // 2), half_width // 2)
+        return pltpu.make_async_remote_copy(
+            src_ref=parts.at[k, h, rows_of(tensor_peer(j)), span],
+            dst_ref=landed.at[k, h, rows_of(j), span],
+            send_sem=rs_send.at[k, h, c, j],
+            recv_sem=rs_recv.at[k, h, c, j],
             device_id={"tensor": tensor_peer(j)},
             device_id_type=MESH,
         )
@@ -488,7 +503,8 @@
         r = lax.rsqrt(over_rows(x * x) + 1e-05)
         d_normed = parts[k, h, rows_of(t)].astype(F32)
         for j in range(1, n_tensor):
-            reduce_copy(k, h, j).wait_recv()
+            for c in range(2):
+                reduce_copy(k, h, c, j).wait_recv()
             d_normed = d_normed + landed[k, h, j * shard : (j + 1) * shard].astype(F32)
         row = gain[slot]
         gains = jnp.concatenate(
@@ -542,10 +558,16 @@
             for r in range(n_tensor):
                 blocks += [side[r * small : (r + 1) * small] for side in sides]
             parts[k, h, :, c * tile : (c + 1) * tile] = jnp.concatenate(blocks, axis=0).astype(BF16)
-
-    def scatter(k, h):
-        for j in others:
-            reduce_copy(k, h, j).start()
+            for j in others:
+                reduce_copy(k, h, c, j).start()
+
+    def prepare(k):
+        slot, micro = 1 - k // 2, 1 - k % 2
+        for h in range(2):
+            base = h * half_rows
+            shares[h, : 2 * (base + half_rows)] = attention_shares(
+                q[slot, micro, base : base + half_rows], kv[slot, micro, : base + half_rows], base
+            )
 
     def step(k, carry):
         slot = 1 - k // 2
@@ -569,7 +591,7 @@
                 q[slot, micro, base : base + half_rows],
                 kv[slot, micro, : base + half_rows],
                 d_attn,
-                base,
+                shares[h, : 2 * (base + half_rows)],
             )
             if h:
                 carried[...] = d_keyval[:half_rows]
@@ -583,7 +605,6 @@
                 @pl.when(jnp.logical_not(tail))
                 def _():
                     project(k, 1, slot, place)
-                    scatter(k, 1)
 
             else:
 
@@ -591,7 +612,6 @@
                 def _():
                     gradient(0)
                     project(k, 1, slot, place)
-                    scatter(k, 1)
 
                 project(k, 0, slot, place)
 
@@ -599,8 +619,6 @@
                 def _():
                     near_phase(0)
 
-                scatter(k, 0)
-
         @pl.when(jnp.logical_and(first, k == 0))
         def _():
             pl.semaphore_signal(go_sem, inc=1, device_id={"section": 1 - s}, device_id_type=MESH)
@@ -620,6 +638,10 @@
             greeted(k)
             greet(k + 1)
 
+        @pl.when(k < 3)
+        def _():
+            prepare(k + 1)
+
         @pl.when(tail)
         def _():
             far_phase(0, 0)
@@ -644,6 +666,7 @@
 
         return carry
 
+    prepare(0)
     lax.fori_loop(0, 4, step, 0)
 
     @pl.when(first)
@@ -693,8 +716,9 @@
     last_phase(0)
     for k in range(4):
         for h in range(2):
-            for j in range(1, n_tensor):
-                reduce_copy(k, h, j).wait_send()
+            for c in range(2):
+                for j in range(1, n_tensor):
+                    reduce_copy(k, h, c, j).wait_send()
     for slot in range(2):
         core_copy(slot).wait_send()
         for part in range(2):
@@ -755,6 +779,7 @@
             pltpu.VMEM((2, items, shard, width // 2), BF16),
             pltpu.VMEM((n_rows // 2, kv_width), F32),
             pltpu.VMEM((2, n_rows // 2, q_width), BF16),
+            pltpu.VMEM((2, 2 * n_rows, q_width // 2), F32),
             pltpu.VMEM((layers, micros * n_rows, kv_width), BF16),
             pltpu.VMEM((layers, 2, width // 2, micros * n_rows), BF16),
             pltpu.VMEM((layers, width // 2, kv_width), BF16),
@@ -768,8 +793,8 @@
             dma((2, n_tensor)),
             dma((items, 2, n_tensor)),
             dma((items, 2, n_tensor)),
-            dma((items, 2, n_tensor)),
-            dma((items, 2, n_tensor)),
+            dma((items, 2, 2, n_tensor)),
+            dma((items, 2, 2, n_tensor)),
             dma((4,)),
             dma((2,)),
             dma((2,)),

time: 127 us -> 128 us (level)
  the two profiles are of different devices: /device:TPU:4 before, /device:TPU:102 now
where the time goes in v5:
time: 128 us
  Pallas kernels  125 us (98%)
  local copies, waits for them, and re-layouts  2.85 us (2%)
    pallas_call x1, Pallas kernels, on_device(): pl.pallas_call(functools.partial(kernel, n_tensor, n_dp), out_shape=(jax....  125 us
    unnamed x2, local copies, waits for them, and re-layouts  2.85 us

profile of v5, /device:TPU:102, one launch (start us, length us, event | category | flops | bytes accessed | tf_op | source)
XLA Modules:
  0.0 128.0 jit_solution(1454551177533637698)
XLA Ops:
  0.6 124.5 %backward.1 = (bf16[16,2048]{1,0:T(8,128)(2,1)}, f32[2,32,128]{2,1,0:T(8,128)}) custom-call(bf16[16,2048]{1,0:T(8,128)(2,1)} %bitcast.19, bf16[2,2,16,2048]{3,2,1,0:T(8,128)(2,1)} %bitcast.16, bf16[2,2,128,2048]{3,2,1,0:T(8,128)(2,1)} %bitcast.12, bf16[2,2,128,256]{3,2,1,0:T(8,128)(2,1)} %bitcast.17, bf16[2,2,128,128]{3,2,1,0:T(8,128)(2,1)} %bitcast.18, ...), custom_call_target="tpu_custom_call" | custom-call | tf_op jit(solution)/shard_map/backward/pallas_call | solution.py:754
  125.2 1.5 %copy.14 = bf16[1,1,16,2048]{3,2,1,0:T(8,128)(2,1)} copy(bf16[1,1,16,2048]{3,2,1,0:T(8,128)(2,1)} %bitcast.20) | data formatting | bytes 131072
  126.6 1.4 %copy.15 = f32[2,1,32,1,128]{4,3,2,1,0:T(1,128)} copy(f32[2,1,32,1,128]{4,3,2,1,0:T(1,128)} %bitcast.21) | data formatting | bytes 65536

commit v6 on v5

--- a/solution.py
+++ b/solution.py
@@ -171,7 +171,7 @@
     ty, tx = t // n_x, lax.rem(t, n_x)
 
     def tensor_peer(j):
-        return lax.rem(ty + j // n_x, 2) * n_x + lax.rem(tx + j % n_x, n_x)
+        return (ty + j // n_x) % 2 * n_x + (tx + j % n_x) % n_x
 
     def distance(j):
         return 2 * (j // n_x) + min(j % n_x, n_x - j % n_x)
@@ -272,13 +272,12 @@
             device_id_type=MESH,
         )
 
-    def reduce_copy(k, h, c, j):
-        span = pl.ds(c * (half_width // 2), half_width // 2)
-        return pltpu.make_async_remote_copy(
-            src_ref=parts.at[k, h, rows_of(tensor_peer(j)), span],
-            dst_ref=landed.at[k, h, rows_of(j), span],
-            send_sem=rs_send.at[k, h, c, j],
-            recv_sem=rs_recv.at[k, h, c, j],
+    def reduce_copy(k, h, j):
+        return pltpu.make_async_remote_copy(
+            src_ref=parts.at[k, h, rows_of(tensor_peer(j))],
+            dst_ref=landed.at[k, h, rows_of(j)],
+            send_sem=rs_send.at[k, h, j],
+            recv_sem=rs_recv.at[k, h, j],
             device_id={"tensor": tensor_peer(j)},
             device_id_type=MESH,
         )
@@ -503,8 +502,7 @@
         r = lax.rsqrt(over_rows(x * x) + 1e-05)
         d_normed = parts[k, h, rows_of(t)].astype(F32)
         for j in range(1, n_tensor):
-            for c in range(2):
-                reduce_copy(k, h, c, j).wait_recv()
+            reduce_copy(k, h, j).wait_recv()
             d_normed = d_normed + landed[k, h, j * shard : (j + 1) * shard].astype(F32)
         row = gain[slot]
         gains = jnp.concatenate(
@@ -558,8 +556,8 @@
             for r in range(n_tensor):
                 blocks += [side[r * small : (r + 1) * small] for side in sides]
             parts[k, h, :, c * tile : (c + 1) * tile] = jnp.concatenate(blocks, axis=0).astype(BF16)
-            for j in others:
-                reduce_copy(k, h, c, j).start()
+        for far, near in zip(others, reversed(others)):
+            reduce_copy(k, h, far * (1 - core) + near * core).start()
 
     def prepare(k):
         slot, micro = 1 - k // 2, 1 - k % 2
@@ -716,9 +714,8 @@
     last_phase(0)
     for k in range(4):
         for h in range(2):
-            for c in range(2):
-                for j in range(1, n_tensor):
-                    reduce_copy(k, h, c, j).wait_send()
+            for j in range(1, n_tensor):
+                reduce_copy(k, h, j).wait_send()
     for slot in range(2):
         core_copy(slot).wait_send()
         for part in range(2):
@@ -793,8 +790,8 @@
             dma((2, n_tensor)),
             dma((items, 2, n_tensor)),
             dma((items, 2, n_tensor)),
-            dma((items, 2, 2, n_tensor)),
-            dma((items, 2, 2, n_tensor)),
+            dma((items, 2, n_tensor)),
+            dma((items, 2, n_tensor)),
             dma((4,)),
             dma((2,)),
             dma((2,)),

time: 128 us -> 127 us (level)
  the two profiles are of different devices: /device:TPU:102 before, /device:TPU:32 now
where the time goes in v6:
time: 127 us
  Pallas kernels  124 us (98%)
  local copies, waits for them, and re-layouts  2.85 us (2%)
    pallas_call x1, Pallas kernels, on_device(): pl.pallas_call(functools.partial(kernel, n_tensor, n_dp), out_shape=(jax....  124 us
    unnamed x2, local copies, waits for them, and re-layouts  2.85 us

profile of v6, /device:TPU:32, one launch (start us, length us, event | category | flops | bytes accessed | tf_op | source)
XLA Modules:
  0.0 127.1 jit_solution(3057919490523668167)
XLA Ops:
  0.6 123.6 %backward.1 = (bf16[16,2048]{1,0:T(8,128)(2,1)}, f32[2,32,128]{2,1,0:T(8,128)}) custom-call(bf16[16,2048]{1,0:T(8,128)(2,1)} %bitcast.19, bf16[2,2,16,2048]{3,2,1,0:T(8,128)(2,1)} %bitcast.16, bf16[2,2,128,2048]{3,2,1,0:T(8,128)(2,1)} %bitcast.12, bf16[2,2,128,256]{3,2,1,0:T(8,128)(2,1)} %bitcast.17, bf16[2,2,128,128]{3,2,1,0:T(8,128)(2,1)} %bitcast.18, ...), custom_call_target="tpu_custom_call" | custom-call | tf_op jit(solution)/shard_map/backward/pallas_call | solution.py:751
  124.2 1.5 %copy.14 = bf16[1,1,16,2048]{3,2,1,0:T(8,128)(2,1)} copy(bf16[1,1,16,2048]{3,2,1,0:T(8,128)(2,1)} %bitcast.20) | data formatting | bytes 131072
  125.7 1.4 %copy.15 = f32[2,1,32,1,128]{4,3,2,1,0:T(1,128)} copy(f32[2,1,32,1,128]{4,3,2,1,0:T(1,128)} %bitcast.21) | data formatting | bytes 65536
